TPU v7x, 512 devices: a whole 4x4x16 slice. The times are simulated.
512 devices in a mesh: item: 8 (over y, x_lo), fsdp: 64 (over z, x_hi, core).
Axes of the slice: x: 4 (x_hi: 2, x_lo: 2; x = x_hi * 2 + x_lo), y: 4, z: 16, core: 2. Of those that a mesh axis runs over, the one named last changes fastest.
Arguments:
- history: bfloat16 [512, 512, 512], P(('item', 'fsdp')), may hold values from -6 to 6
- actions: int32 [512, 512], P(('item', 'fsdp')), may hold values from 0 to 15
- action_table: bfloat16 [16, 512], replicated, may hold values from -3 to 3
- w_in: bfloat16 [2, 512, 2048], P(None, 'fsdp'), may hold values from -0.25 to 0.25
- w_out: bfloat16 [2, 512, 512], P(None, 'fsdp'), may hold values from -0.25 to 0.25
- w_int: bfloat16 [512, 512], P('fsdp'), may hold values from -0.25 to 0.25
- codebook: bfloat16 [32, 256, 16], replicated, may hold values from -0.25 to 0.25
- codes: int32 [128, 128, 32], P('item'), may hold values from 0 to 255
- cand: int32 [512, 4, 8, 4], P(('item', 'fsdp')), may hold values from 0 to 15
- counts: int32 [512, 32], P(('item', 'fsdp')), may hold values from 1 to 4, 80 in all within a row
Outputs:
- scores: float32 [512, 4, 8, 4, 128], P(('item', 'fsdp'))
Inputs may be any that keep to these rules, and one draw needn't show every extreme that they name: `cand`: block numbers within a group; slots at or beyond the count hold ids that are not read. For each user the counts over all 32 columns sum to 80.
All inputs are finite; a program needn't handle non-finite values.
Results may differ from a plain program's by a relative error of at most 0.015.
Values may be sent and summed in bfloat16 or wider, within the bound.
A program may use at most 64 MiB of HBM per device.

v0:
```python
import jax
import jax.numpy as jnp
from jax import lax
from jax.sharding import PartitionSpec as P

HEADS = 4
HD = 128
ACTIONS = 16
LAYERS = 2
SUB = 32
SD = 16
CENT = 256


def layer_norm(value):
    mean = jnp.mean(value, axis=-1, keepdims=True)
    centred = value - mean
    var = jnp.mean(centred * centred, axis=-1, keepdims=True)
    return centred / jnp.sqrt(var + 1e-05)


def build_tables(vectors, codebook):
    count = vectors.shape[0]
    split_vec = vectors.reshape(count, 4, SUB, SD)
    made = jnp.einsum("uksj,scj->uksc", split_vec, codebook, preferred_element_type=jnp.float32)
    return made.astype(jnp.bfloat16).reshape(count, 4, SUB * CENT)


def layer_weights(layer_in, layer_out):
    full_in, full_out = (
        lax.all_gather(layer_in, "fsdp", axis=0, tiled=True),
        lax.all_gather(layer_out, "fsdp", axis=0, tiled=True),
    )
    return (full_in, full_out)


def body(history, actions, action_table, w_in, w_out, w_int, codebook, codes, cand, counts):
    users, length, width = history.shape
    onehot = (actions[:, :, None] == jnp.arange(ACTIONS, dtype=jnp.int32)).astype(jnp.bfloat16)
    x_rows = history.astype(jnp.float32) + jnp.einsum(
        "ula,ad->uld", onehot, action_table, preferred_element_type=jnp.float32
    )
    x_rows = x_rows.reshape(users * length, width)
    rows = jnp.arange(length, dtype=jnp.int32)
    causal = rows[None, :] <= rows[:, None]
    for layer in range(LAYERS):
        full_in, full_out = layer_weights(w_in[layer], w_out[layer])
        normed = layer_norm(x_rows).astype(jnp.bfloat16)
        proj = jax.nn.silu(jnp.dot(normed, full_in, preferred_element_type=jnp.float32)).astype(
            jnp.bfloat16
        )
        proj = proj.reshape(users, length, 4 * width)
        u_part = proj[:, :, 0:width].reshape(users * length, width)
        v_part = proj[:, :, width : 2 * width].reshape(users, length, HEADS, HD)
        q_part = proj[:, :, 2 * width : 3 * width].reshape(users, length, HEADS, HD)
        k_part = proj[:, :, 3 * width : 4 * width].reshape(users, length, HEADS, HD)
        logits = jnp.einsum(
            "uihd,ujhd->uhij", q_part, k_part, preferred_element_type=jnp.float32
        ) / jnp.sqrt(jnp.float32(HD))
        weights = jnp.where(causal[None, None], jax.nn.silu(logits) / length, 0.0).astype(
            jnp.bfloat16
        )
        attn = jnp.einsum(
            "uhij,ujhd->uihd", weights, v_part, preferred_element_type=jnp.float32
        ).reshape(users * length, width)
        gated = (layer_norm(attn) * u_part.astype(jnp.float32)).astype(jnp.bfloat16)
        x_rows = x_rows + jnp.dot(gated, full_out, preferred_element_type=jnp.float32)
    h_rows = layer_norm(x_rows)
    pooled = layer_norm(jnp.mean(h_rows.reshape(users * 4, length // 4, width), axis=1)).astype(
        jnp.bfloat16
    )
    full_int = lax.all_gather(w_int, "fsdp", axis=0, tiled=True)
    interests = (
        jnp.dot(pooled, full_int, preferred_element_type=jnp.float32)
        .astype(jnp.bfloat16)
        .reshape(users, 4, width)
    )
    shaped_counts = counts.reshape(users, 4, cand.shape[2])
    cand_here, count_here = (
        lax.all_to_all(cand, "item", split_axis=2, concat_axis=0, tiled=True),
        lax.all_to_all(shaped_counts, "item", split_axis=2, concat_axis=0, tiled=True),
    )
    tab_all = lax.all_gather(build_tables(interests, codebook), "item", axis=0, tiled=True)
    senders = tab_all.shape[0]
    slots = cand.shape[3]
    total = senders * 4
    tabs = tab_all.reshape(total, SUB * CENT)
    block_ids = cand_here.reshape(total, slots)
    live_count = count_here.reshape(total)

    def one_block(block_codes):
        expanded = (block_codes[:, :, None] == jnp.arange(CENT, dtype=jnp.int32)).astype(
            jnp.bfloat16
        )
        expanded = expanded.reshape(block_codes.shape[0], SUB * CENT)
        return lax.dot_general(
            tabs, expanded, (((1,), (1,)), ((), ())), preferred_element_type=jnp.float32
        )

    every_block = lax.map(one_block, codes)
    every_block = jnp.transpose(every_block, (1, 0, 2))
    values = jnp.take_along_axis(every_block, block_ids[:, :, None], axis=1)
    live = jnp.arange(slots, dtype=jnp.int32)[None, :] < live_count[:, None]
    scored = jnp.where(live[:, :, None], values, 0.0).reshape(senders, 4, 1, slots, codes.shape[1])
    return lax.all_to_all(
        scored.astype(jnp.bfloat16), "item", split_axis=0, concat_axis=2, tiled=True
    ).astype(scored.dtype)


def solution(mesh):
    placed = (
        P(("item", "fsdp"), None, None),
        P(("item", "fsdp"), None),
        P(),
        P(None, "fsdp", None),
        P(None, "fsdp", None),
        P("fsdp", None),
        P(),
        P("item", None, None),
        P(("item", "fsdp"), None, None, None),
        P(("item", "fsdp"), None),
    )
    return jax.shard_map(
        body,
        mesh=mesh,
        in_specs=placed,
        out_specs=P(("item", "fsdp"), None, None, None, None),
        check_vma=False,
    )
```

profile of v0, /device:TPU:1, one launch (start us, length us, event | category | flops | bytes accessed | tf_op | source)
XLA Modules:
  0.0 452.0 jit_solution(15325181090926916055)
XLA Ops:
  6.5 1.4 fusion.61
  8.5 1.3 reduce.12
  10.6 6.0 %all-to-all-start = ((s32[1,4,8]{1,0,2:T(1,128)}), s32[1,4,8]{1,0,2:T(1,128)S(1)}, u32[]{:S(2)}, u32[]{:S(2)}) async-start(s32[1,4,8]{1,0,2:T(1,128)} %copy.62), calls=%async_computation | async-start | bytes 8192 | tf_op jit(solution)/shard_map/all_to_all | solution.py:81
  18.1 1.5 fusion.63
  20.6 90.5 %all-gather.1 = bf16[1,512,512]{2,1,0:T(8,128)(2,1)} all-gather(bf16[1,8,512]{2,1,0:T(8,128)(2,1)S(1)} %get-tuple-element.45), channel_id=3, replica_groups=mesh['item'=8,'fsdp'=64] {'fsdp'}, dimensions={1}, use_global_device_ids=true | all-gather | bytes 532480 | tf_op jit(solution)/shard_map/all_gather | solution.py:32
  111.1 78.3 %all-gather.3 = bf16[1,512,512]{2,1,0:T(8,128)(2,1)} all-gather(bf16[1,8,512]{2,1,0:T(8,128)(2,1)S(1)} %get-tuple-element.44), channel_id=5, replica_groups=mesh['item'=8,'fsdp'=64] {'fsdp'}, dimensions={1}, use_global_device_ids=true | all-gather | bytes 532480 | tf_op jit(solution)/shard_map/all_gather | solution.py:32
  189.4 81.2 %all_gather.22 = bf16[512,512]{1,0:T(8,128)(2,1)} all-gather(bf16[8,512]{1,0:T(8,128)(2,1)S(1)} %copy-done.4), channel_id=1, replica_groups=mesh['item'=8,'fsdp'=64] {'fsdp'}, dimensions={0}, use_global_device_ids=true | all-gather | bytes 532480 | tf_op jit(solution)/shard_map/all_gather | solution.py:72
  271.2 4.8 %all-to-all-start.1 = ((s32[1,4,8,4]{3,1,0,2:T(4,128)}), s32[1,4,8,4]{3,1,0,2:T(4,128)S(1)}, u32[]{:S(2)}, u32[]{:S(2)}) async-start(s32[1,4,8,4]{3,1,0,2:T(4,128)} %copy.65), calls=%async_computation.1 | async-start | bytes 32768 | tf_op jit(solution)/shard_map/all_to_all | solution.py:80
  276.3 4.9 %all-to-all-done.1 = s32[1,4,8,4]{3,1,0,2:T(4,128)S(1)} async-done(((s32[1,4,8,4]{3,1,0,2:T(4,128)}), s32[1,4,8,4]{3,1,0,2:T(4,128)S(1)}, u32[]{:S(2)}, u32[]{:S(2)}) %all-to-all-start.1) | async-done | bytes 544 | tf_op jit(solution)/shard_map/all_to_all | solution.py:80
  281.7 3.3 fusion.7
  285.1 1.3 copy-done.2
  286.9 0.9 reshape.336
  287.8 3.3 fusion.64
  291.6 1.8 fusion.69
  293.7 8.5 %all-gather.9.cloned.1.call-done = bf16[1,512,2048]{2,1,0:T(8,128)(2,1)} async-done(((bf16[1,8,2048]{2,1,0:T(8,128)(2,1)}), bf16[1,512,2048]{2,1,0:T(8,128)(2,1)}) %all-gather.9.cloned.1.call-update) | async-done | bytes 2097168 | tf_op jit(solution)/shard_map/all_gather | solution.py:31
  302.2 3.3 fusion.8
  305.6 1.3 copy-done.1
  307.4 0.9 reshape.341
  308.3 3.8 fusion.70
  314.0 1.9 fusion.75
  317.2 24.8 %all_gather.23 = bf16[8,4,8192]{2,1,0:T(4,128)(2,1)S(1)} all-gather(bf16[1,4,8192]{2,1,0:T(4,128)(2,1)S(1)} %bitcast.155), channel_id=1, replica_groups=mesh['item'=8,'fsdp'=64] {'item'}, dimensions={0}, use_global_device_ids=true | all-gather | bytes 589824 | tf_op jit(solution)/shard_map/all_gather | solution.py:83
  342.1 92.0 %while.10 = (s32[]{:T(128)}, bf16[16,32,128]{2,0,1:T(8,128)(2,1)S(1)}, s32[16,128,32]{1,2,0:T(8,128)}, bf16[32,8192]{1,0:T(8,128)(2,1)S(1)}, s32[]{:T(128)}, /*index=5*/s32[]{:T(128)}) while((s32[]{:T(128)}, bf16[16,32,128]{2,0,1:T(8,128)(2,1)S(1)}, s32[16,128,32]{1,2,0:T(8,128)}, bf16[32,8192]{1,0:T(8,128)(2,1)S(1)}, s32[]{:T(128)}, ...), condition=%wide.region_14.15_spmd, body=%wide.region_13.14_spmd.sunk | while | flops 68157440 | bytes 17563724 | solution.py:100
  343.6 3.3 copy.129
  346.9 0.9 fusion.87
  349.3 3.3 copy.129
  352.7 0.9 fusion.87
  355.1 3.3 copy.129
  358.4 0.9 fusion.87
  360.8 3.3 copy.129
  364.2 0.9 fusion.87
  366.6 3.3 copy.129
  369.9 0.9 fusion.87
  372.3 3.3 copy.129
  378.1 3.3 copy.129
  383.8 3.3 copy.129
  389.6 3.3 copy.129
  392.9 0.9 fusion.87
  395.3 3.3 copy.129
  398.7 0.9 fusion.87
  401.1 3.3 copy.129
  404.4 0.9 fusion.87
  406.8 3.3 copy.129
  412.6 3.3 copy.129
  418.3 3.3 copy.129
  424.1 3.3 copy.129
  429.8 3.3 copy.129
  434.2 1.1 gather_fusion
  435.4 9.0 %all_to_all.39 = bf16[8,4,1,4,128]{4,3,1,2,0:T(4,128)(2,1)S(1)} all-to-all(bf16[8,4,1,4,128]{4,3,1,2,0:T(4,128)(2,1)S(1)} %select_convert_fusion.2), channel_id=1, replica_groups=mesh['item'=8,'fsdp'=64] {'item'}, dimensions={0} | all-to-all | bytes 65536 | tf_op jit(solution)/shard_map/all_to_all | solution.py:105
  (173 shorter events, 42.5 us)
Async XLA Ops:
  6.5 310.5 %copy-start = (bf16[32,256,16]{1,2,0:T(8,128)(2,1)S(1)}, bf16[32,256,16]{1,2,0:T(8,128)(2,1)}, u32[]{:S(2)}) copy-start(bf16[32,256,16]{1,2,0:T(8,128)(2,1)} %param.18) | copy-start | bytes 786436
  6.5 182.8 %copy-start.4 = (bf16[8,512]{1,0:T(8,128)(2,1)S(1)}, bf16[8,512]{1,0:T(8,128)(2,1)}, u32[]{:S(2)}) copy-start(bf16[8,512]{1,0:T(8,128)(2,1)} %param.17) | copy-start | bytes 24580
  6.5 264.0 %copy-start.5 = (s32[1,4,8,4]{2,3,1,0:T(4,128)S(1)}, s32[1,4,8,4]{2,3,1,0:T(4,128)}, u32[]{:S(2)}) copy-start(s32[1,4,8,4]{2,3,1,0:T(4,128)} %param.20) | copy-start | bytes 1540
  6.5 275.2 %all-gather.7.cloned.1.call-start = ((), (), s32[]{:S(2)}) async-start(), calls=%async_computation.3 | async-start | bytes 2129920 | tf_op jit(solution)/shard_map/all_gather | solution.py:31
  10.6 260.6 %all-to-all-start = ((s32[1,4,8]{1,0,2:T(1,128)}), s32[1,4,8]{1,0,2:T(1,128)S(1)}, u32[]{:S(2)}, u32[]{:S(2)}) async-start(s32[1,4,8]{1,0,2:T(1,128)} %copy.62), calls=%async_computation | async-start | bytes 8192 | tf_op jit(solution)/shard_map/all_to_all | solution.py:81
  16.6 285.7 %all-gather.9.cloned.1.call-start = ((), (), s32[]{:S(2)}) async-start(), calls=%async_computation.4 | async-start | bytes 2129920 | tf_op jit(solution)/shard_map/all_gather | solution.py:31
  271.2 9.9 %all-to-all-start.1 = ((s32[1,4,8,4]{3,1,0,2:T(4,128)}), s32[1,4,8,4]{3,1,0,2:T(4,128)S(1)}, u32[]{:S(2)}, u32[]{:S(2)}) async-start(s32[1,4,8,4]{3,1,0,2:T(4,128)} %copy.65), calls=%async_computation.1 | async-start | bytes 32768 | tf_op jit(solution)/shard_map/all_to_all | solution.py:80
  285.1 1.3 copy-start.2
  305.6 1.4 copy-start.1
  313.9 2.8 copy-start.3
Sparse Core Ops, SparseCore 0:
  10.6 149.7 all-gather.6
  163.7 138.4 all-gather.8
where the time goes:
time: 459 us; the launch traced here: 452 us
  blocking collectives  284 us (62%)
  local copies, waits for them, and re-layouts  90.4 us (20%)
  matrix products  33 us (7%)
  waiting for transfers between devices  14.1 us (3%)
  between operations  13.6 us (3%)
  starting transfers between devices  10.8 us (2%)
  other arithmetic  5.37 us (1%)
    all_gather x2, blocking collectives, layer_weights(): lax.all_gather(layer_out, 'fsdp', axis=0, tiled=True)  169 us
    all_gather x1, blocking collectives, body(): full_int = lax.all_gather(w_int, 'fsdp', axis=0, tiled=True)  81.2 us
    while x48, local copies, waits for them, and re-layouts  53.3 us
    all_gather x1, blocking collectives, body(): lax.all_gather(build_tables(interests, codebook), 'item', axis=0, tiled=T...  24.8 us
    eq x48, local copies, waits for them, and re-layouts, one_block(): block_codes[:, :, None] == jnp.arange(CENT, dtype=jnp.int32)  22.8 us
    dot_general x16, matrix products, one_block(): lax.dot_general(tabs, expanded, (((1,), (1,)), ((), ())), preferred_eleme...  13.7 us
  transfers between devices with their start and end apart: 4, of which 2 were waited for; matrix products, arithmetic and copies ran while one was open for 4% of the time, Pallas kernels for 0%

commit v1 on v0

v1 whole, which is shorter than its diff:
```python
import math

import jax
import jax.numpy as jnp
from jax import lax
from jax.experimental import pallas as pl
from jax.experimental.pallas import tpu as pltpu
from jax.sharding import PartitionSpec as P

MESH = pl.DeviceIdType.MESH
F32 = jnp.float32
BF16 = jnp.bfloat16

YS, XL, XH, ZS = 4, 2, 2, 16
XS = XL * XH
ITEMS = YS * XL

D = 512
L = 512
HEADS = 4
HD = 128
ACTIONS = 16
SUB, SD, CENT = 32, 16, 256
NB, BS, CAND, INTR = 16, 128, 4, 4
EPS = 1e-05

IN_BLKS = 16
OUT_BLKS = 4
ALL_BLKS = 2 * IN_BLKS + 3 * OUT_BLKS
Z_OFFS = [8, 7, 9, 6, 10, 5, 11, 4, 12, 3, 13, 2, 14, 1, 15]


def layer_norm(value, eps=EPS):
    mean = jnp.mean(value, axis=-1, keepdims=True)
    centred = value - mean
    var = jnp.mean(centred * centred, axis=-1, keepdims=True)
    return centred * lax.rsqrt(var + eps)


def dot(a, b):
    return lax.dot_general(a, b, (((1,), (0,)), ((), ())), preferred_element_type=F32)


def dot_t(a, b):
    return lax.dot_general(a, b, (((1,), (1,)), ((), ())), preferred_element_type=F32)


def start_values(hist, act, table, x, normed):
    onehot = (
        lax.broadcasted_iota(jnp.int32, (ACTIONS, L), 0) == jnp.broadcast_to(act[...], (ACTIONS, L))
    ).astype(F32)
    rows = 128
    for i in range(L // rows):
        oh = onehot[:, i * rows : (i + 1) * rows].T.astype(BF16)
        part = hist[0, i * rows : (i + 1) * rows].astype(F32) + dot(oh, table[...])
        x[i * rows : (i + 1) * rows] = part
        normed[i * rows : (i + 1) * rows] = layer_norm(part).astype(BF16)


def in_block(weights, layer, blk):
    return weights[layer, blk].reshape(D, 128)


def out_matrix(outs, m):
    return jnp.concatenate([outs[m, j].reshape(D, 128) for j in range(OUT_BLKS)], axis=1)


def project(layer, pair, weights, normed, proj):
    w = jnp.concatenate(
        [in_block(weights, layer, 2 * pair), in_block(weights, layer, 2 * pair + 1)], axis=1
    )
    made = dot(normed[...], w)
    half = 0.5 * made
    made = (half * (1.0 + jnp.tanh(half))).astype(BF16)
    proj[2 * pair] = made[:, :128]
    proj[2 * pair + 1] = made[:, 128:]


def attend(head, proj, attn):
    v, q, k = proj[4 + head], proj[8 + head], proj[12 + head]
    scale = 0.5 / math.sqrt(HD)
    mid = L // 2
    keep = lax.broadcasted_iota(jnp.int32, (mid, mid), 1) <= lax.broadcasted_iota(
        jnp.int32, (mid, mid), 0
    )

    def weigh(qs, ks):
        half = dot_t(qs, ks) * scale
        return 2.0 * half * (0.5 + 0.5 * jnp.tanh(half))

    low = jnp.where(keep, weigh(q[:mid], k[:mid]), 0.0).astype(BF16)
    cross = weigh(q[mid:], k[:mid]).astype(BF16)
    high = jnp.where(keep, weigh(q[mid:], k[mid:]), 0.0).astype(BF16)
    attn[head, :mid] = dot(low, v[:mid])
    attn[head, mid:] = dot(cross, v[:mid]) + dot(high, v[mid:])


def add_out(layer, outs, m, proj, attn, x, normed):
    w = out_matrix(outs, m)
    rows = 128
    for i in range(L // rows):
        r = pl.ds(i * rows, rows)
        a = jnp.concatenate([attn[h, r] for h in range(HEADS)], axis=1)
        u = jnp.concatenate([proj[h, r] for h in range(HEADS)], axis=1)
        gated = (layer_norm(a, EPS * L * L) * u.astype(F32)).astype(BF16)
        new = x[r] + dot(gated, w)
        if layer == 0:
            x[r] = new
            normed[r] = layer_norm(new).astype(BF16)
        else:
            x[r] = layer_norm(new)


def interest_vectors(outs, x):
    per = L // INTR
    rows = [jnp.sum(x[i * per : (i + 1) * per], axis=0, keepdims=True) / per for i in range(INTR)]
    pooled = layer_norm(jnp.concatenate(rows + rows, axis=0))
    pooled = jnp.concatenate([pooled, pooled], axis=0).astype(BF16)
    made = dot(pooled, out_matrix(outs, 2)).astype(BF16).astype(F32)
    return made[: 2 * INTR]


def decode(codes, codebook, cents, decoded):
    eye = (
        lax.broadcasted_iota(jnp.int32, (SD, SD), 0) == lax.broadcasted_iota(jnp.int32, (SD, SD), 1)
    ).astype(BF16)
    for s in range(SUB):
        cents[s] = dot_t(eye, codebook[s])

    @pl.loop(0, NB)
    def _(blk):
        code_t = codes[blk].T
        for s in range(SUB):
            code = jnp.broadcast_to(code_t[s : s + 1], (8, BS))
            spot = code & 127
            made = []
            for part in range(SD // 8):
                r = slice(part * 8, part * 8 + 8)
                low = jnp.take_along_axis(cents[s, r, :128], spot, axis=1)
                high = jnp.take_along_axis(cents[s, r, 128:], spot, axis=1)
                made.append(jnp.where(code < 128, low, high))
            decoded[blk, s * SD : (s + 1) * SD] = jnp.concatenate(made, axis=0).astype(BF16)


def live_slots(cand, counts, mine):
    mine[...] = jnp.zeros_like(mine)
    cnt = jnp.broadcast_to(counts[...], (ITEMS, INTR * ITEMS))
    lane = lax.broadcasted_iota(jnp.int32, (ITEMS, INTR * ITEMS), 1)
    sub = lax.broadcasted_iota(jnp.int32, (ITEMS, INTR * ITEMS), 0)
    slot = lax.broadcasted_iota(jnp.int32, (ITEMS, CAND), 1).astype(F32)
    for k in range(INTR):
        own = jnp.sum(
            jnp.where(lane == k * ITEMS + sub, cnt, 0).astype(F32), axis=1, keepdims=True
        )
        code = jnp.where(slot < own, cand[0, k].astype(F32), -1.0)
        for g in range(ITEMS):
            mine[g, k : k + 1, 0:CAND] = code[g : g + 1]


def kernel(
    hist, act, table, win, wout, wint, codebook, codes, cand, counts,
    out,
    weights, outs, own_rows, got_rows, shard,
    x, normed, proj, attn, cents, decoded,
    slots_mine, slots_got, vec_mine, vec_got, res_mine, res_got,
    ex_s, ex_r, z_s, z_r, p_s, p_r, f_s, f_r, m_s, m_r, i_s, i_r, b_s, b_r,
):
    item, fsdp = lax.axis_index("item"), lax.axis_index("fsdp")
    y, x_lo = item // XL, item % XL
    z, x_hi, c = fsdp // (2 * XH), (fsdp // 2) % XH, fsdp % 2
    zq, zr = z // 4, z % 4
    xx = x_hi * XL + x_lo
    s = c * 2 + x_lo
    partner = (item, fsdp + 1 - 2 * c)

    def z_peer(off):
        return (item, lax.rem(z + off, ZS) * (2 * XH) + x_hi * 2 + c)

    def x_peer(off):
        to = lax.rem(xx + off, XS)
        return (y * XL + to % XL, z * (2 * XH) + (to // XL) * 2 + c)

    def y_peer(off):
        return (lax.rem(y + off, YS) * XL + x_lo, fsdp)

    def item_peer(off):
        return (lax.rem(item + off, ITEMS), fsdp)

    def copy(src, dst, send, recv, to):
        return pltpu.make_async_remote_copy(
            src_ref=src, dst_ref=dst, send_sem=send, recv_sem=recv, device_id=to, device_id_type=MESH
        )

    barrier = pltpu.get_barrier_semaphore()
    met = [partner] + [z_peer(o) for o in range(1, ZS)] + [item_peer(o) for o in range(1, ITEMS)]
    met += [
        (y * XL + lo, z * (2 * XH) + (1 - x_hi) * 2 + c) for lo in range(XL)
    ]
    for peer in met:
        pl.semaphore_signal(barrier, inc=1, device_id=peer, device_id_type=MESH)

    def spread(dst0, ref):
        value = ref.astype(F32)
        for j in range(value.shape[1] // 128):
            own_rows[dst0 + j] = value[:, j * 128 : (j + 1) * 128]

    spread(0, win[0])
    spread(IN_BLKS, win[1])
    spread(2 * IN_BLKS, wout[0])
    spread(2 * IN_BLKS + OUT_BLKS, wout[1])
    spread(2 * IN_BLKS + 2 * OUT_BLKS, wint[...])

    pl.semaphore_wait(barrier, len(met))

    spans = [(0, IN_BLKS), (IN_BLKS, ALL_BLKS)]
    trades = [
        copy(own_rows.at[a:b], got_rows.at[a:b], ex_s.at[i], ex_r.at[i], partner)
        for i, (a, b) in enumerate(spans)
    ]
    for t in trades:
        t.start()

    def assemble(a, b):
        for j in range(a, b):
            mine, theirs = own_rows[j], got_rows[j]
            first = jnp.where(c == 0, mine, theirs)
            second = jnp.where(c == 0, theirs, mine)
            shard[j] = jnp.concatenate([first, second], axis=0).astype(BF16)

    blk = jnp.where(c == 0, y * 2 + x_lo, 8 + x_lo * 4 + y)
    shard_outs = shard.at[2 * IN_BLKS :].reshape(3, OUT_BLKS, 16, 128)

    def z_in(layer, off):
        return copy(
            shard.at[layer * IN_BLKS + blk],
            weights.at[layer, blk, z, x_hi],
            z_s.at[layer, off],
            z_r.at[layer, off],
            z_peer(off),
        )

    def z_out(off):
        return copy(
            shard_outs.at[:, y],
            outs.at[:, y, zq, zr, x_hi],
            z_s.at[2, off],
            z_r.at[2, off],
            z_peer(off),
        )

    def z_out_got(off):
        src = lax.rem(z + ZS - off, ZS)
        ref = outs.at[:, y, src // 4, s, x_hi]
        return copy(ref, ref, z_s.at[2, off], z_r.at[2, off], z_peer(off))

    trades[0].wait_recv()
    assemble(*spans[0])
    for off in Z_OFFS:
        z_in(0, off).start()
    weights[0, blk, z, x_hi] = shard[blk]

    trades[1].wait_recv()
    assemble(*spans[1])

    @pl.when(zr == s)
    def _():
        for off in Z_OFFS:
            z_out(off).start()
        for m in range(3):
            outs[m, y, zq, zr, x_hi] = shard_outs[m, y]

    for off in Z_OFFS:
        z_in(1, off).start()
    weights[1, blk, z, x_hi] = shard[IN_BLKS + blk]

    live_slots(cand, counts, slots_mine)
    slots_got[item] = slots_mine[item]
    slot_copies = [
        copy(
            slots_mine.at[lax.rem(item + o, ITEMS)], slots_got.at[item], m_s.at[o], m_r.at[o], item_peer(o)
        )
        for o in range(1, ITEMS)
    ]
    for t in slot_copies:
        t.start()

    start_values(hist, act, table, x, normed)

    def first_peer(off):
        xp, yp = x_peer(off), y_peer(off)
        return (jnp.where(c == 0, xp[0], yp[0]), jnp.where(c == 0, xp[1], yp[1]))

    def part(chunk):
        if chunk < 2:
            return weights.at[chunk, blk, :, x_hi]
        return outs.at[:, y, :, s, x_hi]

    def step1(chunk, off):
        return copy(part(chunk), part(chunk), p_s.at[chunk, 0, off], p_r.at[chunk, 0, off], first_peer(off))

    def step1_got(chunk, off):
        back_x, back_y = lax.rem(xx + XS - off, XS), lax.rem(y + YS - off, YS)
        lo, hi = back_x % XL, back_x // XL
        f_lo, f_hi = jnp.where(c == 0, lo, x_lo), jnp.where(c == 0, hi, x_hi)
        f_y = jnp.where(c == 0, y, back_y)
        if chunk < 2:
            f_blk = jnp.where(c == 0, f_y * 2 + f_lo, 8 + f_lo * 4 + f_y)
            ref = weights.at[chunk, f_blk, :, f_hi]
        else:
            ref = outs.at[:, f_y, :, c * 2 + f_lo, f_hi]
        return copy(ref, ref, p_s.at[chunk, 0, off], p_r.at[chunk, 0, off], first_peer(off))

    def piece0(chunk, at_y):
        if chunk < 2:
            return weights.at[chunk, pl.ds(at_y * 2, 2)]
        return outs.at[:, at_y, :, 0:2]

    def piece1(chunk, at_x):
        lo, hi = at_x % XL, at_x // XL
        if chunk < 2:
            return weights.at[chunk, pl.ds(8 + lo * 4, 4), :, hi]
        return outs.at[:, :, :, 2 + lo, hi]

    def step2(which, chunk, off, back=False):
        sems = (p_s.at[chunk, 1, off], p_r.at[chunk, 1, off])
        at_y = lax.rem(y + YS - off, YS) if back else y
        at_x = lax.rem(xx + XS - off, XS) if back else xx
        if which == 0:
            return copy(piece0(chunk, at_y), piece0(chunk, at_y), *sems, y_peer(off))
        return copy(piece1(chunk, at_x), piece1(chunk, at_x), *sems, x_peer(off))

    def forward(which, chunk, off):
        sems = (f_s.at[chunk, off], f_r.at[chunk, off])
        at_y, at_x = lax.rem(y + YS - off, YS), lax.rem(xx + XS - off, XS)
        if which == 0:
            return copy(piece0(chunk, at_y), piece0(chunk, at_y), *sems, partner)
        return copy(piece1(chunk, at_x), piece1(chunk, at_x), *sems, partner)

    def after_z(chunk):
        if chunk < 2:
            for off in Z_OFFS:
                z_in(chunk, off).wait_recv()
        else:
            for off in Z_OFFS:
                src = lax.rem(z + ZS - off, ZS)
                pl.when(src % 4 == s)(lambda off=off: z_out_got(off).wait_recv())
        for off in (2, 1, 3):
            step1(chunk, off).start()

    def after_step1(chunk):
        for off in (1, 2, 3):
            step1_got(chunk, off).wait_recv()

        def go(which):
            for off in (2, 1, 3):
                step2(which, chunk, off).start()
            forward(which, chunk, 0).start()

        pl.when(c == 0)(lambda: go(0))
        pl.when(c == 1)(lambda: go(1))

    def after_step2(chunk):
        def go(which):
            for off in (1, 3, 2):
                step2(which, chunk, off, back=True).wait_recv()
                forward(which, chunk, off).start()

        pl.when(c == 0)(lambda: go(0))
        pl.when(c == 1)(lambda: go(1))

    def after_forward(chunk):
        def go(which):
            for off in (0, 1, 3, 2):
                forward(which, chunk, off).wait_recv()

        pl.when(c == 0)(lambda: go(1))
        pl.when(c == 1)(lambda: go(0))

    after_z(0)
    after_z(2)
    after_z(1)
    after_step1(0)
    after_step1(2)
    after_step1(1)

    decode(codes, codebook, cents, decoded)

    after_step2(0)
    after_forward(0)
    for pair in range(8):
        project(0, pair, weights, normed, proj)
    after_step2(2)
    for head in range(HEADS):
        attend(head, proj, attn)
    after_forward(2)
    add_out(0, outs, 0, proj, attn, x, normed)
    after_step2(1)
    after_forward(1)
    for pair in range(8):
        project(1, pair, weights, normed, proj)
    for head in range(HEADS):
        attend(head, proj, attn)
    add_out(1, outs, 1, proj, attn, x, normed)

    vec = interest_vectors(outs, x)
    vec_mine[...] = vec
    vec_copies = [
        copy(vec_mine, vec_got.at[item], i_s.at[o], i_r.at[o], item_peer(o)) for o in range(1, ITEMS)
    ]
    for t in vec_copies:
        t.start()
    vec_got[item] = vec

    def got_from(off):
        return lax.rem(item + ITEMS - off, ITEMS)

    for o in range(1, ITEMS):
        ref = slots_got.at[got_from(o)]
        copy(ref, ref, m_s.at[o], m_r.at[o], item_peer(o)).wait_recv()
    for o in range(1, ITEMS):
        ref = vec_got.at[got_from(o)]
        copy(ref, ref, i_s.at[o], i_r.at[o], item_peer(o)).wait_recv()

    all_vec = vec_got[...].reshape(ITEMS * 8, D).astype(BF16)
    chosen = [[jnp.zeros((8, BS), F32) for _ in range(CAND)] for _ in range(ITEMS)]
    wanted = [
        [jnp.broadcast_to(slots_got[u, :, b : b + 1], (8, BS)) for b in range(CAND)]
        for u in range(ITEMS)
    ]
    for nb in range(NB):
        scored = dot(all_vec, decoded[nb])
        for u in range(ITEMS):
            mine = scored[u * 8 : u * 8 + 8]
            for b in range(CAND):
                chosen[u][b] = jnp.where(wanted[u][b] == float(nb), mine, chosen[u][b])
    for u in range(ITEMS):
        for h in range(CAND // 2):
            res_mine[u, h] = jnp.concatenate(
                [chosen[u][2 * h][:INTR], chosen[u][2 * h + 1][:INTR]], axis=0
            )

    res_copies = [
        copy(
            res_mine.at[lax.rem(item + o, ITEMS)], res_got.at[item], b_s.at[o], b_r.at[o], item_peer(o)
        )
        for o in range(1, ITEMS)
    ]
    for t in res_copies:
        t.start()
    res_got[item] = res_mine[item]

    for t in trades + slot_copies + vec_copies:
        t.wait_send()
    for layer in range(2):
        for off in Z_OFFS:
            z_in(layer, off).wait_send()

    @pl.when(zr == s)
    def _():
        for off in Z_OFFS:
            z_out(off).wait_send()

    for chunk in range(3):
        for off in (1, 2, 3):
            step1(chunk, off).wait_send()

        def go(which, chunk=chunk):
            for off in (1, 2, 3):
                step2(which, chunk, off).wait_send()
            for off in (0, 1, 2, 3):
                forward(which, chunk, off).wait_send()

        pl.when(c == 0)(lambda: go(0))
        pl.when(c == 1)(lambda: go(1))
    for o in range(1, ITEMS):
        ref = res_got.at[got_from(o)]
        copy(ref, ref, b_s.at[o], b_r.at[o], item_peer(o)).wait_recv()
    for t in res_copies:
        t.wait_send()
    out[...] = res_got[...]


def body(history, actions, action_table, w_in, w_out, w_int, codebook, codes, cand, counts):
    vmem = pl.BlockSpec(memory_space=pltpu.VMEM)
    dma = pltpu.SemaphoreType.DMA
    made = pl.pallas_call(
        kernel,
        out_shape=jax.ShapeDtypeStruct((ITEMS, CAND // 2, 2 * INTR, BS), F32),
        in_specs=[vmem] * 10,
        out_specs=vmem,
        scratch_shapes=[
            pltpu.VMEM((2, IN_BLKS, ZS, XH, 16, 128), BF16),
            pltpu.VMEM((3, OUT_BLKS, 4, 4, XH, 16, 128), BF16),
            pltpu.VMEM((ALL_BLKS, 8, 128), F32),
            pltpu.VMEM((ALL_BLKS, 8, 128), F32),
            pltpu.VMEM((ALL_BLKS, 16, 128), BF16),
            pltpu.VMEM((L, D), F32),
            pltpu.VMEM((L, D), BF16),
            pltpu.VMEM((IN_BLKS, L, 128), BF16),
            pltpu.VMEM((HEADS, L, HD), F32),
            pltpu.VMEM((SUB, SD, CENT), F32),
            pltpu.VMEM((NB, D, BS), BF16),
            pltpu.VMEM((ITEMS, 8, 128), F32),
            pltpu.VMEM((ITEMS, 8, 128), F32),
            pltpu.VMEM((8, D), F32),
            pltpu.VMEM((ITEMS, 8, D), F32),
            pltpu.VMEM((ITEMS, CAND // 2, 2 * INTR, BS), F32),
            pltpu.VMEM((ITEMS, CAND // 2, 2 * INTR, BS), F32),
            dma((2,)),
            dma((2,)),
            dma((3, ZS)),
            dma((3, ZS)),
            dma((3, 2, 4)),
            dma((3, 2, 4)),
            dma((3, 4)),
            dma((3, 4)),
            dma((ITEMS,)),
            dma((ITEMS,)),
            dma((ITEMS,)),
            dma((ITEMS,)),
            dma((ITEMS,)),
            dma((ITEMS,)),
        ],
        compiler_params=pltpu.CompilerParams(
            collective_id=0, has_side_effects=True, vmem_limit_bytes=48 * 1024 * 1024
        ),
        name="encode_and_score",
    )(history, actions, action_table, w_in, w_out, w_int, codebook, codes, cand, counts)
    made = made.reshape(ITEMS, CAND, INTR, BS)
    return jnp.transpose(made, (2, 0, 1, 3))[None]


def solution(mesh):
    placed = (
        P(("item", "fsdp"), None, None),
        P(("item", "fsdp"), None),
        P(),
        P(None, "fsdp", None),
        P(None, "fsdp", None),
        P("fsdp", None),
        P(),
        P("item", None, None),
        P(("item", "fsdp"), None, None, None),
        P(("item", "fsdp"), None),
    )
    return jax.shard_map(
        body,
        mesh=mesh,
        in_specs=placed,
        out_specs=P(("item", "fsdp"), None, None, None, None),
        check_vma=False,
    )
```

time: 459 us -> 70.7 us (0.15); the launches traced: 452 us -> 70.5 us
  blocking collectives: 284 us -> 0 us
  local copies, waits for them, and re-layouts: 90.4 us -> 5.74 us
  Pallas kernels: 0 us -> 64.6 us
  matrix products: 33 us -> 0 us
  waiting for transfers between devices: 14.1 us -> 0 us
  between operations: 13.6 us -> 0.11 us
  starting transfers between devices: 10.8 us -> 0 us
  other arithmetic: 5.37 us -> 0 us
    all_gather x4 -> x0, blocking collectives: 275 us -> none  [the longest x2 169 us: layer_weights(): lax.all_gather(layer_out, 'fsdp', axis=0, tiled=True)]
    pallas_call x0 -> x1, Pallas kernels: none -> 64.6 us  [body(): pl.pallas_call(kernel, out_shape=jax.ShapeDtypeStruct((ITEMS, CAND // 2,...]
    while x48 -> x0, local copies, waits for them, and re-layouts: 53.3 us -> none
    dot_general x25 -> x0, matrix products: 33 us -> none  [the longest x16 13.7 us: one_block(): lax.dot_general(tabs, expanded, (((1,), (1,)), ((), ())), preferred_eleme...]
    eq x48 -> x0, local copies, waits for them, and re-layouts: 22.8 us -> none  [one_block(): block_codes[:, :, None] == jnp.arange(CENT, dtype=jnp.int32)]
    all_to_all x2 -> x0, starting transfers between devices: 10.8 us -> none  [the longest x1 5.98 us: body(): lax.all_to_all(shaped_counts, 'item', split_axis=2, concat_axis=0, tiled=...]
    all_to_all x1 -> x0, blocking collectives: 9.05 us -> none  [body(): lax.all_to_all(scored.astype(jnp.bfloat16), 'item', split_axis=0, concat_...]
    all_gather x2 -> x0, waiting for transfers between devices: 8.52 us -> none  [layer_weights(): lax.all_gather(layer_in, 'fsdp', axis=0, tiled=True)]
  transfers between devices with their start and end apart: 4 -> 0, of which waited for: 2 -> 0; matrix products, arithmetic and copies ran while one was open for 4% -> 0% of each run, Pallas kernels for 0% -> 0%
where the time goes in v1:
time: 70.7 us; the launch traced here: 70.5 us
  Pallas kernels  64.6 us (91%)
  local copies, waits for them, and re-layouts  5.74 us (8%)
    pallas_call x1, Pallas kernels, body(): pl.pallas_call(kernel, out_shape=jax.ShapeDtypeStruct((ITEMS, CAND // 2,...  64.6 us
    unnamed x17, local copies, waits for them, and re-layouts  5.09 us

profile of v1, /device:TPU:1, one launch (start us, length us, event | category | flops | bytes accessed | tf_op | source)
XLA Modules:
  0.0 70.5 jit_solution(17895504863571230082)
XLA Ops:
  0.0 0.0 copy-start.6
  0.0 0.0 copy-start.4
  0.0 0.0 copy-start.3
  0.0 0.0 copy-start.1
  0.0 0.0 copy-start.2
  0.0 0.0 copy-start.5
  0.0 0.9 %copy.13.cand = s32[1,4,8,4]{3,2,1,0:T(8,128)S(1)} copy(s32[1,4,8,4]{2,3,1,0:T(4,128)} %param.18) | data formatting | bytes 1024 | tf_op args[8]
  0.9 1.3 %copy.12.codes = s32[16,128,32]{2,1,0:T(8,128)S(1)} copy(s32[16,128,32]{1,2,0:T(8,128)} %param.17) | data formatting | bytes 524288 | tf_op args[7]
  2.2 1.9 %copy.11.codebook = bf16[32,256,16]{2,1,0:T(8,128)(2,1)S(1)} copy(bf16[32,256,16]{1,2,0:T(8,128)(2,1)} %param.16) | data formatting | bytes 524288 | tf_op args[6]
  4.1 0.0 copy-done.6
  4.1 0.0 copy-done.4
  4.1 0.0 copy-done.3
  4.1 0.0 copy-done.1
  4.1 0.0 copy-done.2
  4.1 0.0 copy-done.5
  4.1 0.0 copy-start
  4.2 1.0 %copy-done = bf16[1,512,512]{2,1,0:T(8,128)(2,1)S(1)} copy-done((bf16[1,512,512]{2,1,0:T(8,128)(2,1)S(1)}, bf16[1,512,512]{2,1,0:T(8,128)(2,1)}, u32[]{:S(2)}) %copy-start) | copy-done | bytes 524312
  5.2 64.6 %encode_and_score.1 = f32[8,2,8,128]{3,2,1,0:T(8,128)S(1)} custom-call(bf16[1,512,512]{2,1,0:T(8,128)(2,1)S(1)} %copy-done, s32[1,512]{1,0:T(1,128)S(1)} %copy-done.5, bf16[16,512]{1,0:T(8,128)(2,1)S(1)} %copy-done.2, bf16[2,8,2048]{2,1,0:T(8,128)(2,1)S(1)} %copy-done.1, bf16[2,8,512]{2,1,0:T(8,128)(2,1)S(1)} %copy-done.3, bf16[8,512]{1,0:T(8,128)(2,1)S(1)} %copy-done.4, ...), custom_call_target="tpu_custom_call" | custom-call | tf_op jit(solution)/shard_map/encode_and_score/pallas_call | solution.py:486
  69.8 0.6 copy.16
Async XLA Ops:
  0.0 4.1 %copy-start.6 = (s32[1,32]{1,0:T(1,128)S(1)}, s32[1,32]{1,0:T(1,128)}, u32[]{:S(2)}) copy-start(s32[1,32]{1,0:T(1,128)} %counts.1) | copy-start | bytes 388
  0.0 4.1 %copy-start.4 = (bf16[8,512]{1,0:T(8,128)(2,1)S(1)}, bf16[8,512]{1,0:T(8,128)(2,1)}, u32[]{:S(2)}) copy-start(bf16[8,512]{1,0:T(8,128)(2,1)} %wint.1) | copy-start | bytes 24580
  0.0 4.1 %copy-start.3 = (bf16[2,8,512]{2,1,0:T(8,128)(2,1)S(1)}, bf16[2,8,512]{2,1,0:T(8,128)(2,1)}, u32[]{:S(2)}) copy-start(bf16[2,8,512]{2,1,0:T(8,128)(2,1)} %wout.1) | copy-start | bytes 49156
  0.0 4.1 %copy-start.1 = (bf16[2,8,2048]{2,1,0:T(8,128)(2,1)S(1)}, bf16[2,8,2048]{2,1,0:T(8,128)(2,1)}, u32[]{:S(2)}) copy-start(bf16[2,8,2048]{2,1,0:T(8,128)(2,1)} %win.1) | copy-start | bytes 196612
  0.0 4.1 %copy-start.2 = (bf16[16,512]{1,0:T(8,128)(2,1)S(1)}, bf16[16,512]{1,0:T(8,128)(2,1)}, u32[]{:S(2)}) copy-start(bf16[16,512]{1,0:T(8,128)(2,1)} %table.1) | copy-start | bytes 49156
  0.0 4.1 %copy-start.5 = (s32[1,512]{1,0:T(1,128)S(1)}, s32[1,512]{1,0:T(1,128)}, u32[]{:S(2)}) copy-start(s32[1,512]{1,0:T(1,128)} %act.1) | copy-start | bytes 6148
  4.1 1.0 %copy-start = (bf16[1,512,512]{2,1,0:T(8,128)(2,1)S(1)}, bf16[1,512,512]{2,1,0:T(8,128)(2,1)}, u32[]{:S(2)}) copy-start(bf16[1,512,512]{2,1,0:T(8,128)(2,1)} %hist.1) | copy-start | bytes 1572868

commit v2 on v1

v2 whole, which is shorter than its diff:
```python
import math

import jax
import jax.numpy as jnp
from jax import lax
from jax.experimental import pallas as pl
from jax.experimental.pallas import tpu as pltpu
from jax.sharding import PartitionSpec as P

MESH = pl.DeviceIdType.MESH
F32 = jnp.float32
BF16 = jnp.bfloat16

YS, XL, XH, ZS = 4, 2, 2, 16
XS = XL * XH
ITEMS = YS * XL

D = 512
L = 512
HEADS = 4
HD = 128
ACTIONS = 16
SUB, SD, CENT = 32, 16, 256
NB, BS, CAND, INTR = 16, 128, 4, 4
EPS = 1e-05

IN_BLKS = 16
OUT_BLKS = 4
ALL_BLKS = 2 * IN_BLKS + 3 * OUT_BLKS
ZH = ZS // 2
ORDER = (0, 2, 1)


def layer_norm(value, eps=EPS):
    mean = jnp.mean(value, axis=-1, keepdims=True)
    centred = value - mean
    var = jnp.mean(centred * centred, axis=-1, keepdims=True)
    return centred * lax.rsqrt(var + eps)


def dot(a, b):
    return lax.dot_general(a, b, (((1,), (0,)), ((), ())), preferred_element_type=F32)


def dot_t(a, b):
    return lax.dot_general(a, b, (((1,), (1,)), ((), ())), preferred_element_type=F32)


def start_values(hist, act, table, x, normed):
    onehot = (
        lax.broadcasted_iota(jnp.int32, (ACTIONS, L), 0) == jnp.broadcast_to(act[...], (ACTIONS, L))
    ).astype(F32)
    rows = 128
    for i in range(L // rows):
        oh = onehot[:, i * rows : (i + 1) * rows].T.astype(BF16)
        part = hist[0, i * rows : (i + 1) * rows].astype(F32) + dot(oh, table[...])
        x[i * rows : (i + 1) * rows] = part
        normed[i * rows : (i + 1) * rows] = layer_norm(part).astype(BF16)


def in_block(weights, layer, blk):
    return weights[layer, blk].reshape(D, 128)


def out_matrix(outs, m):
    return jnp.concatenate([outs[m, j].reshape(D, 128) for j in range(OUT_BLKS)], axis=1)


def project(layer, pair, weights, normed, proj):
    w = jnp.concatenate(
        [in_block(weights, layer, 2 * pair), in_block(weights, layer, 2 * pair + 1)], axis=1
    )
    made = dot(normed[...], w)
    half = 0.5 * made
    made = (half * (1.0 + jnp.tanh(half))).astype(BF16)
    proj[2 * pair] = made[:, :128]
    proj[2 * pair + 1] = made[:, 128:]


def attend(head, proj, attn):
    v, q, k = proj[4 + head], proj[8 + head], proj[12 + head]
    scale = 0.5 / math.sqrt(HD)
    mid = L // 2
    keep = lax.broadcasted_iota(jnp.int32, (mid, mid), 1) <= lax.broadcasted_iota(
        jnp.int32, (mid, mid), 0
    )

    def weigh(qs, ks):
        half = dot_t(qs, ks) * scale
        return 2.0 * half * (0.5 + 0.5 * jnp.tanh(half))

    low = jnp.where(keep, weigh(q[:mid], k[:mid]), 0.0).astype(BF16)
    cross = weigh(q[mid:], k[:mid]).astype(BF16)
    high = jnp.where(keep, weigh(q[mid:], k[mid:]), 0.0).astype(BF16)
    attn[head, :mid] = dot(low, v[:mid])
    attn[head, mid:] = dot(cross, v[:mid]) + dot(high, v[mid:])


def add_out(layer, outs, m, proj, attn, x, normed):
    w = out_matrix(outs, m)
    rows = 128
    for i in range(L // rows):
        r = pl.ds(i * rows, rows)
        a = jnp.concatenate([attn[h, r] for h in range(HEADS)], axis=1)
        u = jnp.concatenate([proj[h, r] for h in range(HEADS)], axis=1)
        gated = (layer_norm(a, EPS * L * L) * u.astype(F32)).astype(BF16)
        new = x[r] + dot(gated, w)
        if layer == 0:
            x[r] = new
            normed[r] = layer_norm(new).astype(BF16)
        else:
            x[r] = layer_norm(new)


def interest_vectors(outs, x):
    per = L // INTR
    rows = [jnp.sum(x[i * per : (i + 1) * per], axis=0, keepdims=True) / per for i in range(INTR)]
    pooled = layer_norm(jnp.concatenate([r for r in rows for _ in range(CAND)], axis=0))
    return dot(pooled.astype(BF16), out_matrix(outs, 2)).astype(BF16)


def decode(first, last, codes, codebook, cents, decoded):
    if first == 0:
        for s in range(SUB):
            cents[s] = codebook[s].astype(F32)

    @pl.loop(first, last)
    def _(blk):
        for s in range(SUB):
            code = jnp.broadcast_to(codes[blk, s : s + 1], (8, BS))
            spot = code & 127
            made = []
            for part in range(SD // 8):
                r = slice(part * 8, part * 8 + 8)
                low = jnp.take_along_axis(cents[s, r, :128], spot, axis=1)
                high = jnp.take_along_axis(cents[s, r, 128:], spot, axis=1)
                made.append(jnp.where(code < 128, low, high))
            decoded[blk, s * SD : (s + 1) * SD] = jnp.concatenate(made, axis=0).astype(BF16)


def live_slots(cand, counts, mine):
    mine[...] = jnp.zeros_like(mine)
    cnt = jnp.broadcast_to(counts[...].astype(F32), (CAND, INTR * ITEMS))
    slot = lax.broadcasted_iota(jnp.int32, (CAND, ITEMS), 0).astype(F32)
    rows = []
    for k in range(INTR):
        own = cnt[:, k * ITEMS : (k + 1) * ITEMS]
        rows.append(jnp.where(slot < own, cand[0, k].astype(F32), -1.0))
    mine[:, :ITEMS] = jnp.concatenate(rows, axis=0)


def kernel(
    hist_h, act_h, table_h, win_h, wout_h, wint_h, codebook_h, codes_h, cand_h, counts_h,
    out,
    hist, act, table, win, wout, wint, codebook, codes, cand, counts,
    weights, outs, own_rows, got_rows, shard,
    x, normed, proj, attn, cents, decoded,
    slots_mine, slots_got, wanted, vec_mine, vec_got, res_mine, res_got,
    in_sem, late_sem,
    ex_s, ex_r, z_s, z_r, p1_s, p1_r, p2_s, p2_r, p3_s, f_s, f_r, m_s, m_r, i_s, i_r, b_s, b_r,
):
    item, fsdp = lax.axis_index("item"), lax.axis_index("fsdp")
    y, x_lo = item // XL, item % XL
    z, x_hi, c = fsdp // (2 * XH), (fsdp // 2) % XH, fsdp % 2
    zq, zr = z // 4, z % 4
    half = z // ZH
    xx = x_hi * XL + x_lo
    s = c * 2 + x_lo
    partner = (item, fsdp + 1 - 2 * c)

    def at_z(to):
        return (item, to * (2 * XH) + x_hi * 2 + c)

    def x_peer(off):
        to = lax.rem(xx + off, XS)
        return (y * XL + to % XL, z * (2 * XH) + (to // XL) * 2 + c)

    def y_peer(off):
        return (lax.rem(y + off, YS) * XL + x_lo, fsdp)

    def item_peer(off):
        return (lax.rem(item + off, ITEMS), fsdp)

    def copy(src, dst, send, recv, to):
        return pltpu.make_async_remote_copy(
            src_ref=src, dst_ref=dst, send_sem=send, recv_sem=recv, device_id=to, device_id_type=MESH
        )

    barrier = pltpu.get_barrier_semaphore()
    near = [partner] + [item_peer(o) for o in range(1, ITEMS)]
    near += [(y * XL + lo, z * (2 * XH) + (1 - x_hi) * 2 + c) for lo in range(XL)]
    own_half = [at_z(half * ZH + lax.rem(z + o, ZH)) for o in range(1, ZH)]

    def greet(sem, peers):
        for peer in peers:
            pl.semaphore_signal(sem, inc=1, device_id=peer, device_id_type=MESH)

    operands = [
        (win_h, win), (wout_h, wout), (wint_h, wint), (hist_h, hist), (act_h, act), (table_h, table),
        (codebook_h, codebook), (codes_h, codes), (cand_h, cand), (counts_h, counts),
    ]
    fetches = [pltpu.make_async_copy(h, v, in_sem.at[i]) for i, (h, v) in enumerate(operands)]
    for t in fetches[:3]:
        t.start()
    greet(barrier, near + own_half)

    @pl.when(half == 0)
    def _():
        greet(barrier, [at_z(ZH + t) for t in range(ZH)])

    for t in fetches[3:]:
        t.start()

    def spread(dst0, value):
        value = value.astype(F32)
        for j in range(value.shape[1] // 128):
            own_rows[dst0 + j] = value[:, j * 128 : (j + 1) * 128]

    fetches[0].wait()
    spread(0, win[0])

    def prepare(last):
        for t in fetches[3:]:
            t.wait()
        live_slots(cand, counts, slots_mine)
        start_values(hist, act, table, x, normed)
        decode(0, last, codes, codebook, cents, decoded)

    pl.when(zq == 0)(lambda: prepare(NB))

    @pl.when(half == 0)
    def _():
        pl.semaphore_wait(barrier, len(near) + ZH - 1)

    @pl.when(half == 1)
    def _():
        pl.semaphore_wait(barrier, len(near) + ZS - 1)

    spans = [(0, IN_BLKS), (IN_BLKS, ALL_BLKS)]
    trades = [
        copy(own_rows.at[a:b], got_rows.at[a:b], ex_s.at[i], ex_r.at[i], partner)
        for i, (a, b) in enumerate(spans)
    ]
    trades[0].start()

    @pl.when(half == 1)
    def _():
        greet(late_sem, [at_z(t) for t in range(ZH)])

    spread(IN_BLKS, win[1])
    fetches[1].wait()
    spread(2 * IN_BLKS, wout[0])
    spread(2 * IN_BLKS + OUT_BLKS, wout[1])
    fetches[2].wait()
    spread(2 * IN_BLKS + 2 * OUT_BLKS, wint[...])
    trades[1].start()

    def assemble(a, b):
        for j in range(a, b):
            mine, theirs = own_rows[j], got_rows[j]
            first = jnp.where(c == 0, mine, theirs)
            second = jnp.where(c == 0, theirs, mine)
            shard[j] = jnp.concatenate([first, second], axis=0).astype(BF16)

    blk = jnp.where(c == 0, y * 2 + x_lo, 8 + x_lo * 4 + y)
    shard_outs = shard.at[2 * IN_BLKS :].reshape(3, OUT_BLKS, 16, 128)

    def z_ends(chunk):
        if chunk < 2:
            return shard.at[chunk * IN_BLKS + blk], weights.at[chunk, blk, z, x_hi]
        return shard_outs.at[:, y], outs.at[:, y, zq, zr, x_hi]

    def z_send(chunk, to):
        copy(*z_ends(chunk), z_s.at[chunk], z_r.at[chunk, half], at_z(to)).start()

    def z_keep(chunk):
        src, dst = z_ends(chunk)
        pltpu.make_async_copy(src, dst, z_r.at[chunk, half]).start()

    def if_has(chunk, act):
        if chunk < 2:
            act()
        else:
            pl.when(zr == s)(act)

    def z_near(chunk):
        def act():
            @pl.when(half == 1)
            def _():
                for t in range(ZH):
                    z_send(chunk, t)

            z_keep(chunk)
            for t in range(ZH - 1):
                z_send(chunk, half * ZH + t + jnp.where(t >= z % ZH, 1, 0))

        if_has(chunk, act)

    def z_far(chunk):
        def act():
            for t in range(ZH):
                z_send(chunk, ZH + t)

        if_has(chunk, act)

    def group(chunk, n_in, n_out):
        if chunk < 2:
            return weights.reshape(2 * IN_BLKS * ZS * XH, 16, 128).at[:n_in]
        return outs.reshape(3 * OUT_BLKS * ZS * XH, 16, 128).at[:n_out]

    trades[0].wait_recv()
    assemble(*spans[0])
    z_near(0)
    trades[1].wait_recv()
    assemble(*spans[1])
    z_near(2)
    z_near(1)

    pl.when(zq > 0)(lambda: prepare(NB // 2))

    slots_got[item] = slots_mine[...]
    slot_copies = [
        copy(slots_mine, slots_got.at[item], m_s.at[o], m_r.at[o], item_peer(o))
        for o in range(1, ITEMS)
    ]
    for t in slot_copies:
        t.start()

    def first_peer(off):
        xp, yp = x_peer(off), y_peer(off)
        return (jnp.where(c == 0, xp[0], yp[0]), jnp.where(c == 0, xp[1], yp[1]))

    def part(chunk, h):
        if chunk < 2:
            return weights.at[chunk, blk, pl.ds(h * ZH, ZH), x_hi]
        return outs.at[:, y, pl.ds(h * 2, 2), s, x_hi]

    def piece(which, chunk, h, off):
        if which == 0:
            at_y = lax.rem(y + YS - off, YS)
            if chunk < 2:
                return weights.at[chunk, pl.ds(at_y * 2, 2), pl.ds(h * ZH, ZH)]
            return outs.at[:, at_y, pl.ds(h * 2, 2), 0:2]
        at_x = lax.rem(xx + XS - off, XS)
        lo, hi = at_x % XL, at_x // XL
        if chunk < 2:
            return weights.at[chunk, pl.ds(8 + lo * 4, 4), pl.ds(h * ZH, ZH), hi]
        return outs.at[:, :, pl.ds(h * 2, 2), 2 + lo, hi]

    def piece_part(which, chunk, h, off, n):
        ref = piece(which, chunk, h, off)
        if chunk < 2:
            count = 1 if which == 0 else 2
            return ref.at[n * count : (n + 1) * count]
        return ref.at[:, n] if which == 0 else ref.at[:, :, n]

    def core_half(which, chunk, h):
        if chunk < 2:
            return weights.at[chunk, which * 8 : which * 8 + 8, pl.ds(h * ZH, ZH)]
        return outs.at[:, :, pl.ds(h * 2, 2), which * 2 : which * 2 + 2]

    def by_core(act):
        pl.when(c == 0)(lambda: act(0))
        pl.when(c == 1)(lambda: act(1))

    def after_z(chunk, h):
        ref = part(chunk, h)
        copy(ref, ref, z_s.at[chunk], z_r.at[chunk, h], partner).wait_recv()
        for off in (2, 1, 3):
            copy(ref, ref, p1_s.at[chunk, h], p1_r.at[chunk, h], first_peer(off)).start()

    def after_step1(chunk, h):
        ref = group(chunk, 3 * ZH, 3 * 6)
        copy(ref, ref, p1_s.at[chunk, h], p1_r.at[chunk, h], partner).wait_recv()

        def act(which):
            ref = piece(which, chunk, h, 0)
            peer = y_peer if which == 0 else x_peer
            for off in (1, 3):
                copy(ref, ref, p2_s.at[chunk, h], p2_r.at[chunk, h, off], peer(off)).start()
            copy(ref, ref, f_s.at[chunk, h], f_r.at[chunk, h], partner).start()

        by_core(act)

    def after_near(chunk, h):
        def act(which):
            peer = y_peer if which == 0 else x_peer
            for off in (1, 3):
                ref = piece(which, chunk, h, off)
                copy(ref, ref, p2_s.at[chunk, h], p2_r.at[chunk, h, off], partner).wait_recv()
                on = piece_part(which, chunk, h, off, off // 2)
                copy(on, on, p3_s.at[chunk, h], p2_r.at[chunk, h, 2], peer(off)).start()
                copy(ref, ref, f_s.at[chunk, h], f_r.at[chunk, h], partner).start()

        by_core(act)

    def after_ring(chunk, h):
        def act(which):
            ref = piece(which, chunk, h, 2)
            copy(ref, ref, p3_s.at[chunk, h], p2_r.at[chunk, h, 2], partner).wait_recv()
            copy(ref, ref, f_s.at[chunk, h], f_r.at[chunk, h], partner).start()

        by_core(act)

    def after_forward(chunk, h):
        def act(which):
            ref = core_half(1 - which, chunk, h)
            copy(ref, ref, f_s.at[chunk, h], f_r.at[chunk, h], partner).wait_recv()

        by_core(act)

    own, other = half, 1 - half
    for chunk in ORDER:
        after_z(chunk, own)

    @pl.when(half == 0)
    def _():
        pl.semaphore_wait(late_sem, ZH)
        for chunk in ORDER:
            z_far(chunk)

    for chunk in ORDER:
        after_step1(chunk, own)
    for chunk in ORDER:
        after_z(chunk, other)
    for chunk in ORDER:
        after_near(chunk, own)
    for chunk in ORDER:
        after_step1(chunk, other)
    pl.when(zq > 0)(lambda: decode(NB // 2, NB, codes, codebook, cents, decoded))
    for chunk in ORDER:
        after_ring(chunk, own)

    def got_from(off):
        return lax.rem(item + ITEMS - off, ITEMS)

    for o in range(1, ITEMS):
        ref = slots_got.at[got_from(o)]
        copy(ref, ref, m_s.at[o], m_r.at[o], item_peer(o)).wait_recv()
    rows = ITEMS * INTR * CAND
    lane = lax.broadcasted_iota(jnp.int32, (rows, 128), 1)
    picked = jnp.where(lane == item, slots_got[...].reshape(rows, 128), 0.0)
    wanted[...] = jnp.broadcast_to(jnp.sum(picked, axis=1, keepdims=True), (rows, 128))

    for chunk in ORDER:
        after_near(chunk, other)
    after_ring(0, other)
    after_forward(0, own)
    after_forward(0, other)
    for pair in range(8):
        project(0, pair, weights, normed, proj)
    after_ring(2, other)
    for head in range(HEADS):
        attend(head, proj, attn)
    after_ring(1, other)
    after_forward(2, own)
    after_forward(2, other)
    add_out(0, outs, 0, proj, attn, x, normed)
    after_forward(1, own)
    after_forward(1, other)
    for pair in range(8):
        project(1, pair, weights, normed, proj)
    for head in range(HEADS):
        attend(head, proj, attn)
    add_out(1, outs, 1, proj, attn, x, normed)

    vec = interest_vectors(outs, x)
    vec_mine[...] = vec
    vec_copies = [
        copy(vec_mine, vec_got.at[item], i_s.at[o], i_r.at[o], item_peer(o)) for o in range(1, ITEMS)
    ]
    for t in vec_copies:
        t.start()
    vec_got[item] = vec

    for t in trades + slot_copies:
        t.wait_send()
    for chunk in range(3):

        def sent(chunk=chunk):
            ref = group(chunk, ZS - 1, 3 * (ZS - 1))
            copy(ref, ref, z_s.at[chunk], z_r.at[chunk, 0], partner).wait_send()

        if_has(chunk, sent)
        for h in range(2):
            ref = group(chunk, 3 * ZH, 3 * 6)
            copy(ref, ref, p1_s.at[chunk, h], p1_r.at[chunk, h], partner).wait_send()
            ref = group(chunk, 2 * 4 * ZH, 2 * 24)
            copy(ref, ref, p2_s.at[chunk, h], p2_r.at[chunk, h, 0], partner).wait_send()
            ref = group(chunk, 4 * ZH, 24)
            copy(ref, ref, p3_s.at[chunk, h], p2_r.at[chunk, h, 0], partner).wait_send()
            ref = core_half(0, chunk, h)
            copy(ref, ref, f_s.at[chunk, h], f_r.at[chunk, h], partner).wait_send()

    for o in range(1, ITEMS):
        ref = vec_got.at[got_from(o)]
        copy(ref, ref, i_s.at[o], i_r.at[o], item_peer(o)).wait_recv()

    all_vec = vec_got[...].reshape(rows, D)
    chosen = jnp.zeros((rows, BS), F32)
    for pair in range(NB // 2):
        items = jnp.concatenate([decoded[2 * pair], decoded[2 * pair + 1]], axis=1)
        scored = dot(all_vec, items)
        want = wanted[...]
        chosen = jnp.where(want == float(2 * pair), scored[:, :BS], chosen)
        chosen = jnp.where(want == float(2 * pair + 1), scored[:, BS:], chosen)
    res_mine[...] = chosen.reshape(ITEMS, INTR * CAND, BS)

    res_copies = [
        copy(
            res_mine.at[lax.rem(item + o, ITEMS)], res_got.at[item], b_s.at[o], b_r.at[o], item_peer(o)
        )
        for o in range(1, ITEMS)
    ]
    for t in res_copies:
        t.start()
    res_got[item] = res_mine[item]
    for t in vec_copies:
        t.wait_send()
    for o in range(1, ITEMS):
        ref = res_got.at[got_from(o)]
        copy(ref, ref, b_s.at[o], b_r.at[o], item_peer(o)).wait_recv()
    for t in res_copies:
        t.wait_send()
    out[...] = res_got[...]


def body(history, actions, action_table, w_in, w_out, w_int, codebook, codes, cand, counts):
    hbm = pl.BlockSpec(memory_space=pl.ANY)
    dma = pltpu.SemaphoreType.DMA
    operands = (
        history, actions, action_table, w_in, w_out, w_int,
        jnp.transpose(codebook, (0, 2, 1)),
        jnp.transpose(codes, (0, 2, 1)),
        jnp.transpose(cand, (0, 1, 3, 2)),
        counts,
    )
    made = pl.pallas_call(
        kernel,
        out_shape=jax.ShapeDtypeStruct((ITEMS, INTR * CAND, BS), F32),
        in_specs=[hbm] * 10,
        out_specs=pl.BlockSpec(memory_space=pltpu.VMEM),
        scratch_shapes=[pltpu.VMEM(a.shape, a.dtype) for a in operands]
        + [
            pltpu.VMEM((2, IN_BLKS, ZS, XH, 16, 128), BF16),
            pltpu.VMEM((3, OUT_BLKS, 4, 4, XH, 16, 128), BF16),
            pltpu.VMEM((ALL_BLKS, 8, 128), F32),
            pltpu.VMEM((ALL_BLKS, 8, 128), F32),
            pltpu.VMEM((ALL_BLKS, 16, 128), BF16),
            pltpu.VMEM((L, D), F32),
            pltpu.VMEM((L, D), BF16),
            pltpu.VMEM((IN_BLKS, L, 128), BF16),
            pltpu.VMEM((HEADS, L, HD), F32),
            pltpu.VMEM((SUB, SD, CENT), F32),
            pltpu.VMEM((NB, D, BS), BF16),
            pltpu.VMEM((INTR * CAND, 128), F32),
            pltpu.VMEM((ITEMS, INTR * CAND, 128), F32),
            pltpu.VMEM((ITEMS * INTR * CAND, 128), F32),
            pltpu.VMEM((INTR * CAND, D), BF16),
            pltpu.VMEM((ITEMS, INTR * CAND, D), BF16),
            pltpu.VMEM((ITEMS, INTR * CAND, BS), F32),
            pltpu.VMEM((ITEMS, INTR * CAND, BS), F32),
            dma((len(operands),)),
            pltpu.SemaphoreType.REGULAR,
            dma((2,)),
            dma((2,)),
            dma((3,)),
            dma((3, 2)),
            dma((3, 2)),
            dma((3, 2)),
            dma((3, 2)),
            dma((3, 2, 4)),
            dma((3, 2)),
            dma((3, 2)),
            dma((3, 2)),
            dma((ITEMS,)),
            dma((ITEMS,)),
            dma((ITEMS,)),
            dma((ITEMS,)),
            dma((ITEMS,)),
            dma((ITEMS,)),
        ],
        compiler_params=pltpu.CompilerParams(
            collective_id=0, has_side_effects=True, vmem_limit_bytes=56 * 1024 * 1024
        ),
        name="encode_and_score",
    )(*operands)
    made = made.reshape(ITEMS, INTR, CAND, BS)
    return jnp.transpose(made, (1, 0, 2, 3))[None]


def solution(mesh):
    placed = (
        P(("item", "fsdp"), None, None),
        P(("item", "fsdp"), None),
        P(),
        P(None, "fsdp", None),
        P(None, "fsdp", None),
        P("fsdp", None),
        P(),
        P("item", None, None),
        P(("item", "fsdp"), None, None, None),
        P(("item", "fsdp"), None),
    )
    return jax.shard_map(
        body,
        mesh=mesh,
        in_specs=placed,
        out_specs=P(("item", "fsdp"), None, None, None, None),
        check_vma=False,
    )
```

time: 70.7 us -> 60.3 us (0.85)
  Pallas kernels: 64.6 us -> 58.3 us
  local copies, waits for them, and re-layouts: 5.74 us -> 1.48 us
    pallas_call x1, Pallas kernels: 64.6 us -> 58.3 us  [body(): pl.pallas_call(kernel, out_shape=jax.ShapeDtypeStruct((ITEMS, INTR * CAND...]
    unnamed x17 -> x0, local copies, waits for them, and re-layouts: 5.09 us -> none
    reshape x1, local copies, waits for them, and re-layouts: 0.65 us -> 1.48 us  [body(): made = made.reshape(ITEMS, INTR, CAND, BS)]
where the time goes in v2:
time: 60.3 us; the launch traced here: 59.8 us
  Pallas kernels  58.3 us (97%)
  local copies, waits for them, and re-layouts  1.48 us (2%)
    pallas_call x1, Pallas kernels, body(): pl.pallas_call(kernel, out_shape=jax.ShapeDtypeStruct((ITEMS, INTR * CAND...  58.3 us
    reshape x1, local copies, waits for them, and re-layouts, body(): made = made.reshape(ITEMS, INTR, CAND, BS)  1.48 us

profile of v2, /device:TPU:1, one launch (start us, length us, event | category | flops | bytes accessed | tf_op | source)
XLA Modules:
  0.0 59.8 jit_solution(926874481508316797)
XLA Ops:
  0.0 58.3 %encode_and_score.1 = f32[8,16,128]{2,1,0:T(8,128)} custom-call(bf16[1,512,512]{2,1,0:T(8,128)(2,1)} %hist_h.1, s32[1,512]{1,0:T(1,128)} %act_h.1, bf16[16,512]{1,0:T(8,128)(2,1)} %table_h.1, bf16[2,8,2048]{2,1,0:T(8,128)(2,1)} %win_h.1, bf16[2,8,512]{2,1,0:T(8,128)(2,1)} %wout_h.1, bf16[8,512]{1,0:T(8,128)(2,1)} %wint_h.1, bf16[32,16,256]{2,1,0:T(8,128)(2,1)} %bitcast.10, ...), custom_call_target="tpu_custom_call" | custom-call | tf_op jit(solution)/shard_map/encode_and_score/pallas_call | solution.py:538
  58.3 1.5 %copy.13 = f32[8,4,4,128]{3,2,0,1:T(4,128)} copy(f32[8,4,4,128]{3,2,1,0:T(4,128)} %bitcast.9) | data formatting | bytes 131072 | tf_op jit(solution)/shard_map/reshape | solution.py:588

commit v3 on v2

v3 whole, which is shorter than its diff:
```python
import functools
import math

import jax
import jax.numpy as jnp
from jax import lax
from jax.experimental import pallas as pl
from jax.experimental.pallas import tpu as pltpu
from jax.sharding import PartitionSpec as P

MESH = pl.DeviceIdType.MESH
F32 = jnp.float32
BF16 = jnp.bfloat16

YS, XL, XH, ZS = 4, 2, 2, 16
XS = XL * XH
ITEMS = YS * XL

D = 512
L = 512
HEADS = 4
HD = 128
ACTIONS = 16
SUB, SD, CENT = 32, 16, 256
NB, BS, CAND, INTR = 16, 128, 4, 4
EPS = 1e-05

IN_BLKS = 16
OUT_BLKS = 4
ALL_BLKS = 2 * IN_BLKS + 3 * OUT_BLKS
ZP = 4
IN0, IN1, OUT0, OUT1 = range(4)
ORDER = (IN0, OUT0, IN1, OUT1)
OUT_PART = {OUT0: (0, 1), OUT1: (1, 3)}


def layer_norm(value, eps=EPS):
    mean = jnp.mean(value, axis=-1, keepdims=True)
    centred = value - mean
    var = jnp.mean(centred * centred, axis=-1, keepdims=True)
    return centred * lax.rsqrt(var + eps)


def dot(a, b):
    return lax.dot_general(a, b, (((1,), (0,)), ((), ())), preferred_element_type=F32)


def dot_t(a, b):
    return lax.dot_general(a, b, (((1,), (1,)), ((), ())), preferred_element_type=F32)


def start_values(hist, act, table, x, normed):
    onehot = (
        lax.broadcasted_iota(jnp.int32, (ACTIONS, L), 0) == jnp.broadcast_to(act[...], (ACTIONS, L))
    ).astype(F32)
    rows = 128
    for i in range(L // rows):
        oh = onehot[:, i * rows : (i + 1) * rows].T.astype(BF16)
        part = hist[0, i * rows : (i + 1) * rows].astype(F32) + dot(oh, table[...])
        x[i * rows : (i + 1) * rows] = part
        normed[i * rows : (i + 1) * rows] = layer_norm(part).astype(BF16)


def in_block(weights, layer, blk):
    return weights[layer, blk].reshape(D, 128)


def out_matrix(outs, m):
    return jnp.concatenate([outs[m, j].reshape(D, 128) for j in range(OUT_BLKS)], axis=1)


def project(layer, pair, weights, normed, proj):
    w = jnp.concatenate(
        [in_block(weights, layer, 2 * pair), in_block(weights, layer, 2 * pair + 1)], axis=1
    )
    made = dot(normed[...], w)
    half = 0.5 * made
    made = (half * (1.0 + jnp.tanh(half))).astype(BF16)
    proj[2 * pair] = made[:, :128]
    proj[2 * pair + 1] = made[:, 128:]


def attend(head, proj, attn):
    v, q, k = proj[4 + head], proj[8 + head], proj[12 + head]
    scale = 0.5 / math.sqrt(HD)
    mid = L // 2
    keep = lax.broadcasted_iota(jnp.int32, (mid, mid), 1) <= lax.broadcasted_iota(
        jnp.int32, (mid, mid), 0
    )

    def weigh(qs, ks):
        half = dot_t(qs, ks) * scale
        return 2.0 * half * (0.5 + 0.5 * jnp.tanh(half))

    low = jnp.where(keep, weigh(q[:mid], k[:mid]), 0.0).astype(BF16)
    cross = weigh(q[mid:], k[:mid]).astype(BF16)
    high = jnp.where(keep, weigh(q[mid:], k[mid:]), 0.0).astype(BF16)
    attn[head, :mid] = dot(low, v[:mid])
    attn[head, mid:] = dot(cross, v[:mid]) + dot(high, v[mid:])


def add_out(layer, outs, m, proj, attn, x, normed):
    w = out_matrix(outs, m)
    rows = 128
    for i in range(L // rows):
        r = pl.ds(i * rows, rows)
        a = jnp.concatenate([attn[h, r] for h in range(HEADS)], axis=1)
        u = jnp.concatenate([proj[h, r] for h in range(HEADS)], axis=1)
        gated = (layer_norm(a, EPS * L * L) * u.astype(F32)).astype(BF16)
        new = x[r] + dot(gated, w)
        if layer == 0:
            x[r] = new
            normed[r] = layer_norm(new).astype(BF16)
        else:
            x[r] = layer_norm(new)


def interest_vectors(outs, x):
    per = L // INTR
    rows = [jnp.sum(x[i * per : (i + 1) * per], axis=0, keepdims=True) / per for i in range(INTR)]
    pooled = layer_norm(jnp.concatenate(rows * (D // 128), axis=0))
    made = dot(pooled.astype(BF16), out_matrix(outs, 2))
    row = lax.broadcasted_iota(jnp.int32, (INTR * D // 128, 128), 0) // INTR
    packed = made[:, :128]
    for j in range(1, D // 128):
        packed = jnp.where(row == j, made[:, j * 128 : (j + 1) * 128], packed)
    return packed.astype(BF16)


def slot_rows(expand):
    r = lax.broadcasted_iota(jnp.int32, (128, 128), 0)
    c = lax.broadcasted_iota(jnp.int32, (128, 128), 1)
    same = jnp.logical_and(r // 16 == c // 16, (r // CAND) % INTR == c % INTR)
    for j in range(D // 128):
        expand[j * 128 : (j + 1) * 128] = jnp.where(
            jnp.logical_and(same, (c // INTR) % (D // 128) == j), 1.0, 0.0
        ).astype(BF16)


def decode(first, last, codes, codebook, cents, decoded):
    if first == 0:
        for s in range(SUB):
            cents[s] = codebook[s].astype(F32)

    @pl.loop(first, last)
    def _(blk):
        for s in range(SUB):
            code = jnp.broadcast_to(codes[blk, s : s + 1], (8, BS))
            spot = code & 127
            made = []
            for part in range(SD // 8):
                r = slice(part * 8, part * 8 + 8)
                low = jnp.take_along_axis(cents[s, r, :128], spot, axis=1)
                high = jnp.take_along_axis(cents[s, r, 128:], spot, axis=1)
                made.append(jnp.where(code < 128, low, high))
            decoded[blk, s * SD : (s + 1) * SD] = jnp.concatenate(made, axis=0).astype(BF16)


def live_slots(cand, counts, mine):
    mine[...] = jnp.zeros_like(mine)
    cnt = jnp.broadcast_to(counts[...].astype(F32), (CAND, INTR * ITEMS))
    slot = lax.broadcasted_iota(jnp.int32, (CAND, ITEMS), 0).astype(F32)
    rows = []
    for k in range(INTR):
        own = cnt[:, k * ITEMS : (k + 1) * ITEMS]
        rows.append(jnp.where(slot < own, cand[0, k].astype(F32), -1.0))
    mine[:, :ITEMS] = jnp.concatenate(rows, axis=0)


def kernel(
    hist_h, act_h, table_h, win_h, wout_h, wint_h, codebook_h, codes_h, cand_h, counts_h,
    out,
    hist, act, table, win, wout, wint, codebook, codes, cand, counts,
    weights, outs, own_rows, got_rows, shard,
    x, normed, proj, attn, cents, decoded,
    slots_mine, slots_got, wanted, expand, vec_mine, vec_got, res_mine,
    in_sem, mid_sem, late_sem,
    ex_s, ex_r, z_s, z_r, p_s, p1_r, p2_r, f_r, m_s, m_r, i_s, i_r, b_s, b_r,
):
    item, fsdp = lax.axis_index("item"), lax.axis_index("fsdp")
    y, x_lo = item // XL, item % XL
    z, x_hi, c = fsdp // (2 * XH), (fsdp // 2) % XH, fsdp % 2
    zq, zr = z // 4, z % 4
    xx = x_hi * XL + x_lo
    s = c * 2 + x_lo
    partner = (item, fsdp + 1 - 2 * c)

    def at_z(to):
        return (item, to * (2 * XH) + x_hi * 2 + c)

    def x_peer(off):
        to = lax.rem(xx + off, XS)
        return (y * XL + to % XL, z * (2 * XH) + (to // XL) * 2 + c)

    def y_peer(off):
        return (lax.rem(y + off, YS) * XL + x_lo, fsdp)

    def item_peer(off):
        return (lax.rem(item + off, ITEMS), fsdp)

    def copy(src, dst, send, recv, to):
        return pltpu.make_async_remote_copy(
            src_ref=src, dst_ref=dst, send_sem=send, recv_sem=recv, device_id=to, device_id_type=MESH
        )

    barrier = pltpu.get_barrier_semaphore()
    near = [partner] + [item_peer(o) for o in range(1, ITEMS)]
    near += [(y * XL + lo, z * (2 * XH) + (1 - x_hi) * 2 + c) for lo in range(XL)]
    own_quarter = [at_z(zq * ZP + lax.rem(z + o, ZP)) for o in range(1, ZP)]
    sibling = [at_z((zq + 1 - 2 * (zq % 2)) * ZP + t) for t in range(ZP)]
    planes = [at_z(t) for t in range(ZS)]

    def greet(sem, peers):
        for peer in peers:
            pl.semaphore_signal(sem, inc=1, device_id=peer, device_id_type=MESH)

    def if_quarter(which, act):
        pl.when({0: zq == 0, 1: zq == 1, 2: zq >= 2}[which])(act)

    EARLY, MID, LATE = range(3)

    operands = [
        (win_h, win), (wout_h, wout), (wint_h, wint), (hist_h, hist), (act_h, act), (table_h, table),
        (codebook_h, codebook), (codes_h, codes), (cand_h, cand), (counts_h, counts),
    ]
    fetches = [pltpu.make_async_copy(h, v, in_sem.at[i]) for i, (h, v) in enumerate(operands)]
    for t in fetches[:3]:
        t.start()
    greet(barrier, near + own_quarter)
    if_quarter(EARLY, lambda: greet(barrier, planes[ZP:]))
    if_quarter(MID, lambda: greet(barrier, planes[2 * ZP :]))
    if_quarter(LATE, lambda: greet(barrier, sibling))

    for t in fetches[3:]:
        t.start()

    def spread(dst0, value):
        value = value.astype(F32)
        for j in range(value.shape[1] // 128):
            own_rows[dst0 + j] = value[:, j * 128 : (j + 1) * 128]

    fetches[0].wait()
    spread(0, win[0])

    def prepare(last):
        for t in fetches[3:]:
            t.wait()
        live_slots(cand, counts, slots_mine)
        slot_rows(expand)
        start_values(hist, act, table, x, normed)
        decode(0, last, codes, codebook, cents, decoded)

    first = jnp.logical_and(z <= 1, item + fsdp > 0)
    pl.when(first)(lambda: prepare(NB))
    count = len(near) + ZP - 1
    if_quarter(EARLY, lambda: pl.semaphore_wait(barrier, count))
    if_quarter(MID, lambda: pl.semaphore_wait(barrier, count + ZP))
    if_quarter(LATE, lambda: pl.semaphore_wait(barrier, count + 3 * ZP))

    spans = [(0, IN_BLKS), (IN_BLKS, ALL_BLKS)]
    trades = [
        copy(own_rows.at[a:b], got_rows.at[a:b], ex_s.at[i], ex_r.at[i], partner)
        for i, (a, b) in enumerate(spans)
    ]
    trades[0].start()

    if_quarter(MID, lambda: greet(mid_sem, planes[:ZP]))
    if_quarter(LATE, lambda: greet(late_sem, planes[: 2 * ZP]))

    spread(IN_BLKS, win[1])
    fetches[1].wait()
    spread(2 * IN_BLKS, wout[0])
    spread(2 * IN_BLKS + OUT_BLKS, wout[1])
    fetches[2].wait()
    spread(2 * IN_BLKS + 2 * OUT_BLKS, wint[...])
    trades[1].start()

    def assemble(a, b):
        for j in range(a, b):
            mine, theirs = own_rows[j], got_rows[j]
            first = jnp.where(c == 0, mine, theirs)
            second = jnp.where(c == 0, theirs, mine)
            shard[j] = jnp.concatenate([first, second], axis=0).astype(BF16)

    blk = jnp.where(c == 0, y * 2 + x_lo, 8 + x_lo * 4 + y)
    shard_outs = shard.at[2 * IN_BLKS :].reshape(3, OUT_BLKS, 16, 128)

    def z_ends(chunk):
        if chunk < 2:
            return shard.at[chunk * IN_BLKS + blk], weights.at[chunk, blk, z, x_hi]
        m = slice(*OUT_PART[chunk])
        return shard_outs.at[m, y], outs.at[m, y, zq, zr, x_hi]

    def z_send(chunk, to):
        copy(*z_ends(chunk), z_s.at[chunk], z_r.at[chunk, zq], at_z(to)).start()

    def z_keep(chunk):
        src, dst = z_ends(chunk)
        pltpu.make_async_copy(src, dst, z_r.at[chunk, zq]).start()

    def if_has(chunk, act):
        if chunk < 2:
            act()
        else:
            pl.when(zr == s)(act)

    def z_to(chunk, first, last):
        def act():
            for t in range(first, last):
                z_send(chunk, t)

        if_has(chunk, act)

    def z_near(chunk):
        if_quarter(MID, lambda: z_to(chunk, 0, ZP))
        if_quarter(LATE, lambda: z_to(chunk, 0, 2 * ZP))

        def act():
            z_keep(chunk)
            for t in range(ZP - 1):
                z_send(chunk, zq * ZP + t + jnp.where(t >= zr, 1, 0))

            @pl.when(zq >= 2)
            def _():
                for t in range(ZP):
                    z_send(chunk, (zq + 1 - 2 * (zq % 2)) * ZP + t)

        if_has(chunk, act)

    def group(chunk, n_in, n_out):
        if chunk < 2:
            return weights.reshape(2 * IN_BLKS * ZS * XH, 16, 128).at[:n_in]
        first, last = OUT_PART[chunk]
        return outs.reshape(3 * OUT_BLKS * ZS * XH, 16, 128).at[: n_out * (last - first)]

    trades[0].wait_recv()
    assemble(*spans[0])
    z_near(0)
    pl.when(zq >= 2)(lambda: prepare(NB // 2))
    trades[1].wait_recv()
    assemble(*spans[1])
    for chunk in ORDER[1:]:
        z_near(chunk)

    pl.when(jnp.logical_and(zq <= 1, jnp.logical_not(first)))(lambda: prepare(NB))
    pl.when(zq >= 2)(lambda: decode(NB // 2, NB, codes, codebook, cents, decoded))

    slots_got[item] = slots_mine[...]
    slot_copies = [
        copy(slots_mine, slots_got.at[item], m_s, m_r, item_peer(o))
        for o in range(1, ITEMS)
    ]
    for t in slot_copies:
        t.start()

    def first_peer(off):
        xp, yp = x_peer(off), y_peer(off)
        return (jnp.where(c == 0, xp[0], yp[0]), jnp.where(c == 0, xp[1], yp[1]))

    def part(chunk, q):
        if chunk < 2:
            return weights.at[chunk, blk, pl.ds(q * ZP, ZP), x_hi]
        return outs.at[slice(*OUT_PART[chunk]), y, q, s, x_hi]

    def piece(which, chunk, q, off):
        if which == 0:
            at_y = lax.rem(y + YS - off, YS)
            if chunk < 2:
                return weights.at[chunk, pl.ds(at_y * 2, 2), pl.ds(q * ZP, ZP)]
            return outs.at[slice(*OUT_PART[chunk]), at_y, q, 0:2]
        at_x = lax.rem(xx + XS - off, XS)
        lo, hi = at_x % XL, at_x // XL
        if chunk < 2:
            return weights.at[chunk, pl.ds(8 + lo * 4, 4), pl.ds(q * ZP, ZP), hi]
        return outs.at[slice(*OUT_PART[chunk]), :, q, 2 + lo, hi]

    def piece_part(which, chunk, q, off, n):
        ref = piece(which, chunk, q, off)
        if chunk < 2:
            many = 1 if which == 0 else 2
            return ref.at[n * many : (n + 1) * many]
        return ref.at[:, n] if which == 0 else ref.at[:, 2 * n : 2 * n + 2]

    def core_half(which, chunk, q):
        if chunk < 2:
            return weights.at[chunk, which * 8 : which * 8 + 8, pl.ds(q * ZP, ZP)]
        return outs.at[slice(*OUT_PART[chunk]), :, q, which * 2 : which * 2 + 2]

    def by_core(act):
        pl.when(c == 0)(lambda: act(0))
        pl.when(c == 1)(lambda: act(1))

    def after_z(chunk, q):
        ref = part(chunk, q)
        copy(ref, ref, p_s.at[chunk], z_r.at[chunk, q], partner).wait_recv()
        for off in (2, 1, 3):
            copy(ref, ref, p_s.at[chunk], p1_r.at[chunk, q], first_peer(off)).start()

    def after_step1(chunk, q, ring=False):
        ref = group(chunk, 3 * ZP, 3)
        copy(ref, ref, p_s.at[chunk], p1_r.at[chunk, q], partner).wait_recv()

        def act(which):
            ref = piece(which, chunk, q, 0)
            peer = y_peer if which == 0 else x_peer
            for off in (1, 3) if ring else (2, 1, 3):
                copy(ref, ref, p_s.at[chunk], p2_r.at[chunk, q, off - 1], peer(off)).start()
            copy(ref, ref, p_s.at[chunk], f_r.at[chunk, q], partner).start()

        by_core(act)

    def pass_on(which, chunk, q, off):
        ref = piece(which, chunk, q, off)
        copy(ref, ref, p_s.at[chunk], p2_r.at[chunk, q, off - 1], partner).wait_recv()
        copy(ref, ref, p_s.at[chunk], f_r.at[chunk, q], partner).start()

    def after_step2(chunk, q):
        def act(which):
            for off in (1, 3, 2):
                pass_on(which, chunk, q, off)

        by_core(act)

    def after_near(chunk, q):
        def act(which):
            peer = y_peer if which == 0 else x_peer
            for off in (1, 3):
                pass_on(which, chunk, q, off)
                on = piece_part(which, chunk, q, off, off // 2)
                copy(on, on, p_s.at[chunk], p2_r.at[chunk, q, 1], peer(off)).start()

        by_core(act)

    def after_far(chunk, q):
        by_core(lambda which: pass_on(which, chunk, q, 2))

    def after_forward(chunk):
        for q in range(ZS // ZP):

            def act(which, q=q):
                ref = core_half(1 - which, chunk, q)
                copy(ref, ref, p_s.at[chunk], f_r.at[chunk, q], partner).wait_recv()

            by_core(act)

    q0, q1 = zq, zq + 1 - 2 * (zq % 2)
    q2 = 2 * (1 - zq // 2)

    def each(act, *pairs):
        for q, chunk in pairs:
            act(chunk, q)

    def z_of(*pairs):
        each(after_z, *pairs)

    def step1_of(*pairs):
        each(after_step1, *pairs)

    def ring1_of(*pairs):
        each(functools.partial(after_step1, ring=True), *pairs)

    def step2_of(*pairs):
        each(after_step2, *pairs)

    def near_of(*pairs):
        each(after_near, *pairs)

    def far_of(*pairs):
        each(after_far, *pairs)

    own = [(q0, chunk) for chunk in ORDER]
    sib = [(q1, chunk) for chunk in ORDER]

    def both(chunk):
        return (q0, chunk), (q1, chunk)

    def half(chunk):
        return (q2, chunk), (q2 + 1, chunk)

    def late_rows():
        pl.semaphore_wait(late_sem, 2 * ZP)
        z_to(IN0, 2 * ZP, ZS)

    @pl.when(zq <= 1)
    def _():
        z_of(*own)

        @pl.when(zq == 0)
        def _():
            pl.semaphore_wait(mid_sem, ZP)
            for chunk in ORDER:
                z_to(chunk, ZP, 2 * ZP)

        pl.when(zq == 1)(late_rows)
        ring1_of(*own)
        z_of(*sib)
        pl.when(zq == 0)(late_rows)
        near_of(*own)
        for chunk in ORDER[1:]:
            z_to(chunk, 2 * ZP, ZS)
        z_of(*half(IN0))
        ring1_of(*sib)
        far_of(*own)
        step1_of(*half(IN0))
        z_of(*half(OUT0))
        near_of(*sib)
        z_of(*half(IN1))
        step1_of(*half(OUT0))
        far_of((q1, IN0), (q1, OUT0))
        step2_of(*half(IN0))
        step1_of(*half(IN1))
        far_of((q1, IN1), (q1, OUT1))

    @pl.when(zq >= 2)
    def _():
        z_of(*both(IN0))
        z_of(*both(OUT0))
        step1_of(*both(IN0))
        z_of(*both(IN1))
        ring1_of(*both(OUT0))
        z_of(*half(IN0))
        step2_of(*both(IN0))
        ring1_of(*both(IN1))
        near_of(*both(OUT0))
        z_of(*both(OUT1))
        step1_of(*half(IN0))
        z_of(*half(OUT0))
        far_of(*both(OUT0))
        near_of(*both(IN1))
        z_of(*half(IN1))
        step1_of(*half(OUT0))
        ring1_of(*both(OUT1))
        step2_of(*half(IN0))
        far_of(*both(IN1))
        step1_of(*half(IN1))
        near_of(*both(OUT1))

    def all_got(got, sem):
        ref = got.at[: ITEMS - 1]
        copy(ref, ref, p_s.at[0], sem, partner).wait_recv()

    all_got(slots_got, m_r)
    rows = ITEMS * INTR * CAND
    lane = lax.broadcasted_iota(jnp.int32, (rows, 128), 1)
    picked = jnp.where(lane == item, slots_got[...].reshape(rows, 128), 0.0)
    wanted[...] = jnp.broadcast_to(jnp.sum(picked, axis=1, keepdims=True), (rows, 128))

    after_forward(IN0)
    for pair in range(8):
        project(0, pair, weights, normed, proj)
    z_of(*half(OUT1))
    step2_of(*half(OUT0))
    for head in range(HEADS):
        attend(head, proj, attn)
    step1_of(*half(OUT1))
    after_forward(OUT0)
    add_out(0, outs, 0, proj, attn, x, normed)
    step2_of(*half(IN1))
    after_forward(IN1)
    for pair in range(8):
        project(1, pair, weights, normed, proj)
    pl.when(zq >= 2)(lambda: far_of(*both(OUT1)))
    step2_of(*half(OUT1))
    for head in range(HEADS):
        attend(head, proj, attn)
    after_forward(OUT1)
    add_out(1, outs, 1, proj, attn, x, normed)

    vec = interest_vectors(outs, x)
    vec_mine[...] = vec
    vec_copies = [
        copy(vec_mine, vec_got.at[item], i_s, i_r, item_peer(o)) for o in range(1, ITEMS)
    ]
    for t in vec_copies:
        t.start()
    vec_got[item] = vec

    def all_left(sent, sem):
        ref = sent.at[: ITEMS - 1]
        copy(ref, ref, sem, i_r, partner).wait_send()

    for t in trades:
        t.wait_send()
    all_left(slots_got, m_s)
    for chunk in range(4):

        def left(chunk=chunk):
            ref = group(chunk, ZS - 1, ZS - 1)
            copy(ref, ref, z_s.at[chunk], i_r, partner).wait_send()

        if_has(chunk, left)
        ref = group(chunk, 4 * 124, 4 * 31)
        copy(ref, ref, p_s.at[chunk], i_r, partner).wait_send()

    all_got(vec_got, i_r)
    spread_out = dot(expand[...], vec_got[...].reshape(128, 128)).astype(BF16)
    all_vec = jnp.concatenate([spread_out[j * rows : (j + 1) * rows] for j in range(D // 128)], axis=1)
    chosen = jnp.zeros((rows, BS), F32)
    for pair in range(NB // 2):
        items = jnp.concatenate([decoded[2 * pair], decoded[2 * pair + 1]], axis=1)
        scored = dot(all_vec, items)
        want = wanted[...]
        chosen = jnp.where(want == float(2 * pair), scored[:, :BS], chosen)
        chosen = jnp.where(want == float(2 * pair + 1), scored[:, BS:], chosen)
    res_mine[...] = chosen.reshape(ITEMS, INTR * CAND, BS)

    for o in range(1, ITEMS):
        to = lax.rem(item + o, ITEMS)
        copy(res_mine.at[to], out.at[item], b_s, b_r, item_peer(o)).start()
    pltpu.make_async_copy(res_mine.at[item], out.at[item], b_r).start()
    all_left(vec_got, i_s)
    copy(out, out, b_s, b_r, partner).wait_recv()
    all_left(res_mine, b_s)


def body(history, actions, action_table, w_in, w_out, w_int, codebook, codes, cand, counts):
    hbm = pl.BlockSpec(memory_space=pltpu.HBM)
    dma = pltpu.SemaphoreType.DMA
    operands = (
        history, actions, action_table, w_in, w_out, w_int,
        jnp.transpose(codebook, (0, 2, 1)),
        jnp.transpose(codes, (0, 2, 1)),
        jnp.transpose(cand, (0, 1, 3, 2)),
        counts,
    )
    made = pl.pallas_call(
        kernel,
        out_shape=jax.ShapeDtypeStruct((ITEMS, INTR * CAND, BS), F32),
        in_specs=[hbm] * 10,
        out_specs=hbm,
        scratch_shapes=[pltpu.VMEM(a.shape, a.dtype) for a in operands]
        + [
            pltpu.VMEM((2, IN_BLKS, ZS, XH, 16, 128), BF16),
            pltpu.VMEM((3, OUT_BLKS, 4, 4, XH, 16, 128), BF16),
            pltpu.VMEM((ALL_BLKS, 8, 128), F32),
            pltpu.VMEM((ALL_BLKS, 8, 128), F32),
            pltpu.VMEM((ALL_BLKS, 16, 128), BF16),
            pltpu.VMEM((L, D), F32),
            pltpu.VMEM((L, D), BF16),
            pltpu.VMEM((IN_BLKS, L, 128), BF16),
            pltpu.VMEM((HEADS, L, HD), F32),
            pltpu.VMEM((SUB, SD, CENT), F32),
            pltpu.VMEM((NB, D, BS), BF16),
            pltpu.VMEM((INTR * CAND, 128), F32),
            pltpu.VMEM((ITEMS, INTR * CAND, 128), F32),
            pltpu.VMEM((ITEMS * INTR * CAND, 128), F32),
            pltpu.VMEM((D, 128), BF16),
            pltpu.VMEM((16, 128), BF16),
            pltpu.VMEM((ITEMS, 16, 128), BF16),
            pltpu.VMEM((ITEMS, INTR * CAND, BS), F32),
            dma((len(operands),)),
            pltpu.SemaphoreType.REGULAR,
            pltpu.SemaphoreType.REGULAR,
            dma((2,)),
            dma((2,)),
            dma((4,)),
            dma((4, 4)),
            dma((4,)),
            dma((4, 4)),
            dma((4, 4, 3)),
            dma((4, 4)),
        ]
        + [dma(())] * 6,
        compiler_params=pltpu.CompilerParams(
            collective_id=0, has_side_effects=True, vmem_limit_bytes=56 * 1024 * 1024
        ),
        name="encode_and_score",
    )(*operands)
    made = made.reshape(ITEMS, INTR, CAND, BS)
    return jnp.transpose(made, (1, 0, 2, 3))[None]


def solution(mesh):
    placed = (
        P(("item", "fsdp"), None, None),
        P(("item", "fsdp"), None),
        P(),
        P(None, "fsdp", None),
        P(None, "fsdp", None),
        P("fsdp", None),
        P(),
        P("item", None, None),
        P(("item", "fsdp"), None, None, None),
        P(("item", "fsdp"), None),
    )
    return jax.shard_map(
        body,
        mesh=mesh,
        in_specs=placed,
        out_specs=P(("item", "fsdp"), None, None, None, None),
        check_vma=False,
    )
```

time: 60.3 us -> 58.5 us (0.970)
  the two profiles are of different devices: /device:TPU:1 before, /device:TPU:480 now
where the time goes in v3:
time: 58.5 us; the launch traced here: 58.3 us
  Pallas kernels  56.8 us (97%)
  local copies, waits for them, and re-layouts  1.48 us (3%)
    pallas_call x1, Pallas kernels, body(): pl.pallas_call(kernel, out_shape=jax.ShapeDtypeStruct((ITEMS, INTR * CAND...  56.8 us
    reshape x1, local copies, waits for them, and re-layouts, body(): made = made.reshape(ITEMS, INTR, CAND, BS)  1.48 us

profile of v3, /device:TPU:480, one launch (start us, length us, event | category | flops | bytes accessed | tf_op | source)
XLA Modules:
  0.0 58.3 jit_solution(10578517193754609364)
XLA Ops:
  0.0 56.8 %encode_and_score.1 = f32[8,16,128]{2,1,0:T(8,128)} custom-call(bf16[1,512,512]{2,1,0:T(8,128)(2,1)} %hist_h.1, s32[1,512]{1,0:T(1,128)} %act_h.1, bf16[16,512]{1,0:T(8,128)(2,1)} %table_h.1, bf16[2,8,2048]{2,1,0:T(8,128)(2,1)} %win_h.1, bf16[2,8,512]{2,1,0:T(8,128)(2,1)} %wout_h.1, bf16[8,512]{1,0:T(8,128)(2,1)} %wint_h.1, bf16[32,16,256]{2,1,0:T(8,128)(2,1)} %bitcast.10, ...), custom_call_target="tpu_custom_call" | custom-call | tf_op jit(solution)/shard_map/encode_and_score/pallas_call | solution.py:626
  56.9 1.5 %copy.13 = f32[8,4,4,128]{3,2,0,1:T(4,128)} copy(f32[8,4,4,128]{3,2,1,0:T(4,128)} %bitcast.9) | data formatting | bytes 131072 | tf_op jit(solution)/shard_map/reshape | solution.py:669

commit v4 on v3

--- a/solution.py
+++ b/solution.py
@@ -115,56 +115,44 @@
             x[r] = layer_norm(new)
 
 
-def interest_vectors(outs, x):
+def make_tables(outs, x, codebook, tables):
     per = L // INTR
     rows = [jnp.sum(x[i * per : (i + 1) * per], axis=0, keepdims=True) / per for i in range(INTR)]
-    pooled = layer_norm(jnp.concatenate(rows * (D // 128), axis=0))
-    made = dot(pooled.astype(BF16), out_matrix(outs, 2))
-    row = lax.broadcasted_iota(jnp.int32, (INTR * D // 128, 128), 0) // INTR
-    packed = made[:, :128]
-    for j in range(1, D // 128):
-        packed = jnp.where(row == j, made[:, j * 128 : (j + 1) * 128], packed)
-    return packed.astype(BF16)
-
-
-def slot_rows(expand):
-    r = lax.broadcasted_iota(jnp.int32, (128, 128), 0)
-    c = lax.broadcasted_iota(jnp.int32, (128, 128), 1)
-    same = jnp.logical_and(r // 16 == c // 16, (r // CAND) % INTR == c % INTR)
-    for j in range(D // 128):
-        expand[j * 128 : (j + 1) * 128] = jnp.where(
-            jnp.logical_and(same, (c // INTR) % (D // 128) == j), 1.0, 0.0
-        ).astype(BF16)
-
-
-def decode(first, last, codes, codebook, cents, decoded):
-    if first == 0:
-        for s in range(SUB):
-            cents[s] = codebook[s].astype(F32)
-
-    @pl.loop(first, last)
-    def _(blk):
-        for s in range(SUB):
-            code = jnp.broadcast_to(codes[blk, s : s + 1], (8, BS))
-            spot = code & 127
-            made = []
-            for part in range(SD // 8):
-                r = slice(part * 8, part * 8 + 8)
-                low = jnp.take_along_axis(cents[s, r, :128], spot, axis=1)
-                high = jnp.take_along_axis(cents[s, r, 128:], spot, axis=1)
-                made.append(jnp.where(code < 128, low, high))
-            decoded[blk, s * SD : (s + 1) * SD] = jnp.concatenate(made, axis=0).astype(BF16)
-
-
-def live_slots(cand, counts, mine):
-    mine[...] = jnp.zeros_like(mine)
-    cnt = jnp.broadcast_to(counts[...].astype(F32), (CAND, INTR * ITEMS))
-    slot = lax.broadcasted_iota(jnp.int32, (CAND, ITEMS), 0).astype(F32)
-    rows = []
+    pooled = layer_norm(jnp.concatenate(rows + rows, axis=0)).astype(BF16)
+    interests = dot(pooled, out_matrix(outs, 2)).astype(BF16).astype(F32)
+    sub = lax.broadcasted_iota(jnp.int32, (SUB, D), 0)
+    feature = lax.broadcasted_iota(jnp.int32, (SUB, D), 1)
+    apart = jnp.concatenate(
+        [
+            jnp.where(feature // SD == sub, jnp.broadcast_to(interests[k : k + 1], (SUB, D)), 0.0)
+            for k in range(INTR)
+        ],
+        axis=0,
+    ).astype(BF16)
+    made = dot(apart, codebook[...].reshape(SUB * SD, CENT))
+    tables[...] = made.astype(BF16).astype(F32)
+
+
+def score(tables, codes_all, cand, counts, out):
     for k in range(INTR):
-        own = cnt[:, k * ITEMS : (k + 1) * ITEMS]
-        rows.append(jnp.where(slot < own, cand[0, k].astype(F32), -1.0))
-    mine[:, :ITEMS] = jnp.concatenate(rows, axis=0)
+        low = [tables[k * SUB + 8 * i : k * SUB + 8 * i + 8, :128] for i in range(SUB // 8)]
+        high = [tables[k * SUB + 8 * i : k * SUB + 8 * i + 8, 128:] for i in range(SUB // 8)]
+        for g in range(ITEMS):
+            live = counts[0, k * ITEMS + g]
+            for b in range(CAND):
+                blk = g * NB + jnp.clip(cand[0, k, b, g], 0, NB - 1)
+                total = None
+                for i in range(SUB // 8):
+                    code = codes_all[blk, 8 * i : 8 * i + 8]
+                    spot = code & 127
+                    value = jnp.where(
+                        code < 128,
+                        jnp.take_along_axis(low[i], spot, axis=1),
+                        jnp.take_along_axis(high[i], spot, axis=1),
+                    )
+                    total = value if total is None else total + value
+                scored = jnp.sum(total, axis=0, keepdims=True)
+                out[k, g, b : b + 1] = jnp.where(b < live, scored, 0.0)
 
 
 def kernel(
@@ -172,10 +160,9 @@
     out,
     hist, act, table, win, wout, wint, codebook, codes, cand, counts,
     weights, outs, own_rows, got_rows, shard,
-    x, normed, proj, attn, cents, decoded,
-    slots_mine, slots_got, wanted, expand, vec_mine, vec_got, res_mine,
+    x, normed, proj, attn, codes_got, codes_all, tables,
     in_sem, mid_sem, late_sem,
-    ex_s, ex_r, z_s, z_r, p_s, p1_r, p2_r, f_r, m_s, m_r, i_s, i_r, b_s, b_r,
+    ex_s, ex_r, z_s, z_r, p_s, p1_r, p2_r, f_r, c_s, c_r,
 ):
     item, fsdp = lax.axis_index("item"), lax.axis_index("fsdp")
     y, x_lo = item // XL, item % XL
@@ -195,17 +182,13 @@
     def y_peer(off):
         return (lax.rem(y + off, YS) * XL + x_lo, fsdp)
 
-    def item_peer(off):
-        return (lax.rem(item + off, ITEMS), fsdp)
-
     def copy(src, dst, send, recv, to):
         return pltpu.make_async_remote_copy(
             src_ref=src, dst_ref=dst, send_sem=send, recv_sem=recv, device_id=to, device_id_type=MESH
         )
 
     barrier = pltpu.get_barrier_semaphore()
-    near = [partner] + [item_peer(o) for o in range(1, ITEMS)]
-    near += [(y * XL + lo, z * (2 * XH) + (1 - x_hi) * 2 + c) for lo in range(XL)]
+    near = [partner] + [x_peer(o) for o in range(1, XS)] + [y_peer(o) for o in range(1, YS)]
     own_quarter = [at_z(zq * ZP + lax.rem(z + o, ZP)) for o in range(1, ZP)]
     sibling = [at_z((zq + 1 - 2 * (zq % 2)) * ZP + t) for t in range(ZP)]
     planes = [at_z(t) for t in range(ZS)]
@@ -242,16 +225,14 @@
     fetches[0].wait()
     spread(0, win[0])
 
-    def prepare(last):
+    def prepare():
         for t in fetches[3:]:
             t.wait()
-        live_slots(cand, counts, slots_mine)
-        slot_rows(expand)
+        codes_got[y, x_lo, pl.ds(c * 8, 8)] = codes[pl.ds(c * 8, 8)].astype(F32).astype(BF16)
         start_values(hist, act, table, x, normed)
-        decode(0, last, codes, codebook, cents, decoded)
 
     first = jnp.logical_and(z <= 1, item + fsdp > 0)
-    pl.when(first)(lambda: prepare(NB))
+    pl.when(first)(prepare)
     count = len(near) + ZP - 1
     if_quarter(EARLY, lambda: pl.semaphore_wait(barrier, count))
     if_quarter(MID, lambda: pl.semaphore_wait(barrier, count + ZP))
@@ -313,7 +294,6 @@
 
     def z_near(chunk):
         if_quarter(MID, lambda: z_to(chunk, 0, ZP))
-        if_quarter(LATE, lambda: z_to(chunk, 0, 2 * ZP))
 
         def act():
             z_keep(chunk)
@@ -326,6 +306,7 @@
                     z_send(chunk, (zq + 1 - 2 * (zq % 2)) * ZP + t)
 
         if_has(chunk, act)
+        if_quarter(LATE, lambda: z_to(chunk, 0, 2 * ZP))
 
     def group(chunk, n_in, n_out):
         if chunk < 2:
@@ -336,22 +317,63 @@
     trades[0].wait_recv()
     assemble(*spans[0])
     z_near(0)
-    pl.when(zq >= 2)(lambda: prepare(NB // 2))
+    pl.when(zq >= 2)(prepare)
     trades[1].wait_recv()
     assemble(*spans[1])
     for chunk in ORDER[1:]:
         z_near(chunk)
 
-    pl.when(jnp.logical_and(zq <= 1, jnp.logical_not(first)))(lambda: prepare(NB))
-    pl.when(zq >= 2)(lambda: decode(NB // 2, NB, codes, codebook, cents, decoded))
-
-    slots_got[item] = slots_mine[...]
-    slot_copies = [
-        copy(slots_mine, slots_got.at[item], m_s, m_r, item_peer(o))
-        for o in range(1, ITEMS)
-    ]
-    for t in slot_copies:
-        t.start()
+    pl.when(jnp.logical_and(zq <= 1, jnp.logical_not(first)))(prepare)
+
+    other_lo = (item + 1 - 2 * x_lo, fsdp)
+
+    def codes_copy(ref, to, stage):
+        return copy(ref, ref, c_s, c_r.at[stage], to)
+
+    def codes_first():
+        @pl.when(c == 0)
+        def _():
+            codes_copy(codes_got.at[y, x_lo, 0:8], other_lo, 0).start()
+
+        @pl.when(c == 1)
+        def _():
+            for off in (2, 1, 3):
+                codes_copy(codes_got.at[y, x_lo, 8:16], y_peer(off), 0).start()
+
+    def codes_second():
+        @pl.when(c == 0)
+        def _():
+            codes_copy(codes_got.at[y, 1 - x_lo, 0:8], partner, 0).wait_recv()
+            for off in (2, 1, 3):
+                codes_copy(codes_got.at[y, :, 0:8], y_peer(off), 1).start()
+
+        @pl.when(c == 1)
+        def _():
+            codes_copy(codes_got.at[0:3, 0, 8:16], partner, 0).wait_recv()
+            codes_copy(codes_got.at[:, x_lo, 8:16], other_lo, 1).start()
+
+    def codes_third():
+        @pl.when(c == 0)
+        def _():
+            codes_copy(codes_got.at[0:3, :, 0:8], partner, 1).wait_recv()
+            codes_copy(codes_got.at[:, :, 0:8], partner, 2).start()
+
+        @pl.when(c == 1)
+        def _():
+            codes_copy(codes_got.at[:, 0, 8:16], partner, 1).wait_recv()
+            codes_copy(codes_got.at[:, :, 8:16], partner, 2).start()
+
+    def codes_last():
+        pl.when(c == 0)(lambda: codes_copy(codes_got.at[:, :, 8:16], partner, 2).wait_recv())
+        pl.when(c == 1)(lambda: codes_copy(codes_got.at[:, :, 0:8], partner, 2).wait_recv())
+        for at_y in range(YS):
+            for lo in range(XL):
+
+                @pl.loop(0, NB)
+                def _(i, at_y=at_y, lo=lo):
+                    codes_all[(at_y * XL + lo) * NB + i] = codes_got[at_y, lo, i].astype(F32).astype(jnp.int32)
+
+    codes_first()
 
     def first_peer(off):
         xp, yp = x_peer(off), y_peer(off)
@@ -484,6 +506,7 @@
     @pl.when(zq <= 1)
     def _():
         z_of(*own)
+        codes_second()
 
         @pl.when(zq == 0)
         def _():
@@ -495,122 +518,92 @@
         ring1_of(*own)
         z_of(*sib)
         pl.when(zq == 0)(late_rows)
+        codes_third()
         near_of(*own)
+        z_of(*half(IN0))
+        ring1_of(*sib)
         for chunk in ORDER[1:]:
             z_to(chunk, 2 * ZP, ZS)
-        z_of(*half(IN0))
-        ring1_of(*sib)
         far_of(*own)
+        codes_last()
         step1_of(*half(IN0))
         z_of(*half(OUT0))
         near_of(*sib)
         z_of(*half(IN1))
         step1_of(*half(OUT0))
+        step1_of(*half(IN1))
         far_of((q1, IN0), (q1, OUT0))
         step2_of(*half(IN0))
-        step1_of(*half(IN1))
+        z_of(*half(OUT1))
         far_of((q1, IN1), (q1, OUT1))
 
-    @pl.when(zq >= 2)
+    def if_late(act):
+        pl.when(zq >= 2)(act)
+
+    @if_late
     def _():
         z_of(*both(IN0))
         z_of(*both(OUT0))
         step1_of(*both(IN0))
         z_of(*both(IN1))
         ring1_of(*both(OUT0))
-        z_of(*half(IN0))
         step2_of(*both(IN0))
         ring1_of(*both(IN1))
+        z_of(*half(IN0))
         near_of(*both(OUT0))
         z_of(*both(OUT1))
+        near_of(*both(IN1))
         step1_of(*half(IN0))
+        far_of(*both(OUT0))
         z_of(*half(OUT0))
-        far_of(*both(OUT0))
-        near_of(*both(IN1))
         z_of(*half(IN1))
+        ring1_of(*both(OUT1))
+        far_of(*both(IN1))
         step1_of(*half(OUT0))
-        ring1_of(*both(OUT1))
+        step1_of(*half(IN1))
         step2_of(*half(IN0))
-        far_of(*both(IN1))
-        step1_of(*half(IN1))
         near_of(*both(OUT1))
-
-    def all_got(got, sem):
-        ref = got.at[: ITEMS - 1]
-        copy(ref, ref, p_s.at[0], sem, partner).wait_recv()
-
-    all_got(slots_got, m_r)
-    rows = ITEMS * INTR * CAND
-    lane = lax.broadcasted_iota(jnp.int32, (rows, 128), 1)
-    picked = jnp.where(lane == item, slots_got[...].reshape(rows, 128), 0.0)
-    wanted[...] = jnp.broadcast_to(jnp.sum(picked, axis=1, keepdims=True), (rows, 128))
+        codes_second()
+        z_of(*half(OUT1))
 
     after_forward(IN0)
     for pair in range(8):
         project(0, pair, weights, normed, proj)
-    z_of(*half(OUT1))
     step2_of(*half(OUT0))
+    if_late(lambda: far_of(*both(OUT1)))
     for head in range(HEADS):
         attend(head, proj, attn)
     step1_of(*half(OUT1))
+    step2_of(*half(IN1))
     after_forward(OUT0)
     add_out(0, outs, 0, proj, attn, x, normed)
-    step2_of(*half(IN1))
+    if_late(codes_third)
     after_forward(IN1)
     for pair in range(8):
         project(1, pair, weights, normed, proj)
-    pl.when(zq >= 2)(lambda: far_of(*both(OUT1)))
     step2_of(*half(OUT1))
     for head in range(HEADS):
         attend(head, proj, attn)
+    if_late(codes_last)
     after_forward(OUT1)
     add_out(1, outs, 1, proj, attn, x, normed)
 
-    vec = interest_vectors(outs, x)
-    vec_mine[...] = vec
-    vec_copies = [
-        copy(vec_mine, vec_got.at[item], i_s, i_r, item_peer(o)) for o in range(1, ITEMS)
-    ]
-    for t in vec_copies:
-        t.start()
-    vec_got[item] = vec
-
-    def all_left(sent, sem):
-        ref = sent.at[: ITEMS - 1]
-        copy(ref, ref, sem, i_r, partner).wait_send()
+    make_tables(outs, x, codebook, tables)
+    score(tables, codes_all, cand, counts, out)
 
     for t in trades:
         t.wait_send()
-    all_left(slots_got, m_s)
+    ref = codes_got.reshape(ITEMS * NB, SUB, BS).at[: 15 * 8]
+    copy(ref, ref, c_s, c_r.at[0], partner).wait_send()
     for chunk in range(4):
 
         def left(chunk=chunk):
             ref = group(chunk, ZS - 1, ZS - 1)
-            copy(ref, ref, z_s.at[chunk], i_r, partner).wait_send()
+            copy(ref, ref, z_s.at[chunk], c_r.at[0], partner).wait_send()
 
         if_has(chunk, left)
         ref = group(chunk, 4 * 124, 4 * 31)
-        copy(ref, ref, p_s.at[chunk], i_r, partner).wait_send()
-
-    all_got(vec_got, i_r)
-    spread_out = dot(expand[...], vec_got[...].reshape(128, 128)).astype(BF16)
-    all_vec = jnp.concatenate([spread_out[j * rows : (j + 1) * rows] for j in range(D // 128)], axis=1)
-    chosen = jnp.zeros((rows, BS), F32)
-    for pair in range(NB // 2):
-        items = jnp.concatenate([decoded[2 * pair], decoded[2 * pair + 1]], axis=1)
-        scored = dot(all_vec, items)
-        want = wanted[...]
-        chosen = jnp.where(want == float(2 * pair), scored[:, :BS], chosen)
-        chosen = jnp.where(want == float(2 * pair + 1), scored[:, BS:], chosen)
-    res_mine[...] = chosen.reshape(ITEMS, INTR * CAND, BS)
-
-    for o in range(1, ITEMS):
-        to = lax.rem(item + o, ITEMS)
-        copy(res_mine.at[to], out.at[item], b_s, b_r, item_peer(o)).start()
-    pltpu.make_async_copy(res_mine.at[item], out.at[item], b_r).start()
-    all_left(vec_got, i_s)
-    copy(out, out, b_s, b_r, partner).wait_recv()
-    all_left(res_mine, b_s)
+        copy(ref, ref, p_s.at[chunk], c_r.at[0], partner).wait_send()
 
 
 def body(history, actions, action_table, w_in, w_out, w_int, codebook, codes, cand, counts):
@@ -625,10 +618,11 @@
     )
     made = pl.pallas_call(
         kernel,
-        out_shape=jax.ShapeDtypeStruct((ITEMS, INTR * CAND, BS), F32),
+        out_shape=pltpu.VMEM((INTR, ITEMS, CAND, BS), F32),
         in_specs=[hbm] * 10,
-        out_specs=hbm,
-        scratch_shapes=[pltpu.VMEM(a.shape, a.dtype) for a in operands]
+        out_specs=pl.BlockSpec(memory_space=pltpu.VMEM),
+        scratch_shapes=[pltpu.VMEM(a.shape, a.dtype) for a in operands[:8]]
+        + [pltpu.SMEM(a.shape, a.dtype) for a in operands[8:]]
         + [
             pltpu.VMEM((2, IN_BLKS, ZS, XH, 16, 128), BF16),
             pltpu.VMEM((3, OUT_BLKS, 4, 4, XH, 16, 128), BF16),
@@ -639,15 +633,9 @@
             pltpu.VMEM((L, D), BF16),
             pltpu.VMEM((IN_BLKS, L, 128), BF16),
             pltpu.VMEM((HEADS, L, HD), F32),
-            pltpu.VMEM((SUB, SD, CENT), F32),
-            pltpu.VMEM((NB, D, BS), BF16),
-            pltpu.VMEM((INTR * CAND, 128), F32),
-            pltpu.VMEM((ITEMS, INTR * CAND, 128), F32),
-            pltpu.VMEM((ITEMS * INTR * CAND, 128), F32),
-            pltpu.VMEM((D, 128), BF16),
-            pltpu.VMEM((16, 128), BF16),
-            pltpu.VMEM((ITEMS, 16, 128), BF16),
-            pltpu.VMEM((ITEMS, INTR * CAND, BS), F32),
+            pltpu.VMEM((YS, XL, NB, SUB, BS), BF16),
+            pltpu.VMEM((ITEMS * NB, SUB, BS), jnp.int32),
+            pltpu.VMEM((INTR * SUB, CENT), F32),
             dma((len(operands),)),
             pltpu.SemaphoreType.REGULAR,
             pltpu.SemaphoreType.REGULAR,
@@ -659,15 +647,15 @@
             dma((4, 4)),
             dma((4, 4, 3)),
             dma((4, 4)),
-        ]
-        + [dma(())] * 6,
+            dma(()),
+            dma((3,)),
+        ],
         compiler_params=pltpu.CompilerParams(
             collective_id=0, has_side_effects=True, vmem_limit_bytes=56 * 1024 * 1024
         ),
         name="encode_and_score",
     )(*operands)
-    made = made.reshape(ITEMS, INTR, CAND, BS)
-    return jnp.transpose(made, (1, 0, 2, 3))[None]
+    return made[None]
 
 
 def solution(mesh):

time: 58.5 us -> 51.3 us (0.88)
  the two profiles are of different devices: /device:TPU:480 before, /device:TPU:449 now
where the time goes in v4:
time: 51.3 us; the launch traced here: 51.2 us
  Pallas kernels  50.5 us (98%)
  local copies, waits for them, and re-layouts  0.63 us (1%)
    pallas_call x1, Pallas kernels, body(): pl.pallas_call(kernel, out_shape=pltpu.VMEM((INTR, ITEMS, CAND, BS), F32)...  50.5 us

profile of v4, /device:TPU:449, one launch (start us, length us, event | category | flops | bytes accessed | tf_op | source)
XLA Modules:
  0.0 51.2 jit_solution(14416584317539792325)
XLA Ops:
  0.0 50.5 %encode_and_score.1 = f32[4,8,4,128]{3,2,1,0:T(4,128)S(1)} custom-call(bf16[1,512,512]{2,1,0:T(8,128)(2,1)} %hist_h.1, s32[1,512]{1,0:T(1,128)} %act_h.1, bf16[16,512]{1,0:T(8,128)(2,1)} %table_h.1, bf16[2,8,2048]{2,1,0:T(8,128)(2,1)} %win_h.1, bf16[2,8,512]{2,1,0:T(8,128)(2,1)} %wout_h.1, bf16[8,512]{1,0:T(8,128)(2,1)} %wint_h.1, ...), custom_call_target="tpu_custom_call" | custom-call | tf_op jit(solution)/shard_map/encode_and_score/pallas_call | solution.py:619
  50.5 0.6 %copy.12 = f32[1,4,8,4,128]{4,3,2,1,0:T(4,128)} copy(f32[1,4,8,4,128]{4,3,2,1,0:T(4,128)S(1)} %bitcast.4) | data formatting | bytes 131072

commit v5 on v4

--- a/solution.py
+++ b/solution.py
@@ -90,7 +90,7 @@
 
     def weigh(qs, ks):
         half = dot_t(qs, ks) * scale
-        return 2.0 * half * (0.5 + 0.5 * jnp.tanh(half))
+        return half * (1.0 + jnp.tanh(half))
 
     low = jnp.where(keep, weigh(q[:mid], k[:mid]), 0.0).astype(BF16)
     cross = weigh(q[mid:], k[:mid]).astype(BF16)
@@ -133,17 +133,18 @@
     tables[...] = made.astype(BF16).astype(F32)
 
 
-def score(tables, codes_all, cand, counts, out):
+def score(tables, codes, cand, counts, out):
     for k in range(INTR):
         low = [tables[k * SUB + 8 * i : k * SUB + 8 * i + 8, :128] for i in range(SUB // 8)]
         high = [tables[k * SUB + 8 * i : k * SUB + 8 * i + 8, 128:] for i in range(SUB // 8)]
         for g in range(ITEMS):
             live = counts[0, k * ITEMS + g]
             for b in range(CAND):
-                blk = g * NB + jnp.clip(cand[0, k, b, g], 0, NB - 1)
+                blk = jnp.clip(cand[0, k, b, g], 0, NB - 1)
+                item_codes = codes[g // XL, g % XL, blk].astype(F32).astype(jnp.int32)
                 total = None
                 for i in range(SUB // 8):
-                    code = codes_all[blk, 8 * i : 8 * i + 8]
+                    code = item_codes[8 * i : 8 * i + 8]
                     spot = code & 127
                     value = jnp.where(
                         code < 128,
@@ -160,7 +161,7 @@
     out,
     hist, act, table, win, wout, wint, codebook, codes, cand, counts,
     weights, outs, own_rows, got_rows, shard,
-    x, normed, proj, attn, codes_got, codes_all, tables,
+    x, normed, proj, attn, codes_got, tables,
     in_sem, mid_sem, late_sem,
     ex_s, ex_r, z_s, z_r, p_s, p1_r, p2_r, f_r, c_s, c_r,
 ):
@@ -366,12 +367,6 @@
     def codes_last():
         pl.when(c == 0)(lambda: codes_copy(codes_got.at[:, :, 8:16], partner, 2).wait_recv())
         pl.when(c == 1)(lambda: codes_copy(codes_got.at[:, :, 0:8], partner, 2).wait_recv())
-        for at_y in range(YS):
-            for lo in range(XL):
-
-                @pl.loop(0, NB)
-                def _(i, at_y=at_y, lo=lo):
-                    codes_all[(at_y * XL + lo) * NB + i] = codes_got[at_y, lo, i].astype(F32).astype(jnp.int32)
 
     codes_first()
 
@@ -503,10 +498,11 @@
         pl.semaphore_wait(late_sem, 2 * ZP)
         z_to(IN0, 2 * ZP, ZS)
 
+    codes_second()
+
     @pl.when(zq <= 1)
     def _():
         z_of(*own)
-        codes_second()
 
         @pl.when(zq == 0)
         def _():
@@ -525,7 +521,6 @@
         for chunk in ORDER[1:]:
             z_to(chunk, 2 * ZP, ZS)
         far_of(*own)
-        codes_last()
         step1_of(*half(IN0))
         z_of(*half(OUT0))
         near_of(*sib)
@@ -547,49 +542,49 @@
         step1_of(*both(IN0))
         z_of(*both(IN1))
         ring1_of(*both(OUT0))
+        codes_third()
         step2_of(*both(IN0))
         ring1_of(*both(IN1))
         z_of(*half(IN0))
         near_of(*both(OUT0))
         z_of(*both(OUT1))
+        step1_of(*half(IN0))
         near_of(*both(IN1))
-        step1_of(*half(IN0))
         far_of(*both(OUT0))
         z_of(*half(OUT0))
         z_of(*half(IN1))
         ring1_of(*both(OUT1))
-        far_of(*both(IN1))
         step1_of(*half(OUT0))
         step1_of(*half(IN1))
+        z_of(*half(OUT1))
+        far_of(*both(IN1))
         step2_of(*half(IN0))
-        near_of(*both(OUT1))
-        codes_second()
-        z_of(*half(OUT1))
 
     after_forward(IN0)
     for pair in range(8):
         project(0, pair, weights, normed, proj)
+
+    if_late(lambda: near_of(*both(OUT1)))
     step2_of(*half(OUT0))
-    if_late(lambda: far_of(*both(OUT1)))
     for head in range(HEADS):
         attend(head, proj, attn)
     step1_of(*half(OUT1))
     step2_of(*half(IN1))
     after_forward(OUT0)
     add_out(0, outs, 0, proj, attn, x, normed)
-    if_late(codes_third)
     after_forward(IN1)
     for pair in range(8):
         project(1, pair, weights, normed, proj)
+    if_late(lambda: far_of(*both(OUT1)))
     step2_of(*half(OUT1))
     for head in range(HEADS):
         attend(head, proj, attn)
-    if_late(codes_last)
+    codes_last()
     after_forward(OUT1)
     add_out(1, outs, 1, proj, attn, x, normed)
 
     make_tables(outs, x, codebook, tables)
-    score(tables, codes_all, cand, counts, out)
+    score(tables, codes_got, cand, counts, out)
 
     for t in trades:
         t.wait_send()
@@ -634,7 +629,6 @@
             pltpu.VMEM((IN_BLKS, L, 128), BF16),
             pltpu.VMEM((HEADS, L, HD), F32),
             pltpu.VMEM((YS, XL, NB, SUB, BS), BF16),
-            pltpu.VMEM((ITEMS * NB, SUB, BS), jnp.int32),
             pltpu.VMEM((INTR * SUB, CENT), F32),
             dma((len(operands),)),
             pltpu.SemaphoreType.REGULAR,

time: 51.3 us -> 49 us (0.955)
  the two profiles are of different devices: /device:TPU:449 before, /device:TPU:1 now
where the time goes in v5:
time: 49 us; the launch traced here: 48.9 us
  Pallas kernels  48.3 us (99%)
  local copies, waits for them, and re-layouts  0.63 us (1%)
    pallas_call x1, Pallas kernels, body(): pl.pallas_call(kernel, out_shape=pltpu.VMEM((INTR, ITEMS, CAND, BS), F32)...  48.3 us

profile of v5, /device:TPU:1, one launch (start us, length us, event | category | flops | bytes accessed | tf_op | source)
XLA Modules:
  0.0 48.9 jit_solution(6093079383429801986)
XLA Ops:
  0.0 48.3 %encode_and_score.1 = f32[4,8,4,128]{3,2,1,0:T(4,128)S(1)} custom-call(bf16[1,512,512]{2,1,0:T(8,128)(2,1)} %hist_h.1, s32[1,512]{1,0:T(1,128)} %act_h.1, bf16[16,512]{1,0:T(8,128)(2,1)} %table_h.1, bf16[2,8,2048]{2,1,0:T(8,128)(2,1)} %win_h.1, bf16[2,8,512]{2,1,0:T(8,128)(2,1)} %wout_h.1, bf16[8,512]{1,0:T(8,128)(2,1)} %wint_h.1, ...), custom_call_target="tpu_custom_call" | custom-call | tf_op jit(solution)/shard_map/encode_and_score/pallas_call | solution.py:614
  48.3 0.6 %copy.12 = f32[1,4,8,4,128]{4,3,2,1,0:T(4,128)} copy(f32[1,4,8,4,128]{4,3,2,1,0:T(4,128)S(1)} %bitcast.4) | data formatting | bytes 131072

commit v6 on v5

--- a/solution.py
+++ b/solution.py
@@ -101,7 +101,8 @@
 
 def add_out(layer, outs, m, proj, attn, x, normed):
     w = out_matrix(outs, m)
-    rows = 128
+    rows = L // INTR
+    means = []
     for i in range(L // rows):
         r = pl.ds(i * rows, rows)
         a = jnp.concatenate([attn[h, r] for h in range(HEADS)], axis=1)
@@ -112,12 +113,11 @@
             x[r] = new
             normed[r] = layer_norm(new).astype(BF16)
         else:
-            x[r] = layer_norm(new)
-
-
-def make_tables(outs, x, codebook, tables):
-    per = L // INTR
-    rows = [jnp.sum(x[i * per : (i + 1) * per], axis=0, keepdims=True) / per for i in range(INTR)]
+            means.append(jnp.sum(layer_norm(new), axis=0, keepdims=True) / rows)
+    return means
+
+
+def make_tables(outs, rows, codebook, tables):
     pooled = layer_norm(jnp.concatenate(rows + rows, axis=0)).astype(BF16)
     interests = dot(pooled, out_matrix(outs, 2)).astype(BF16).astype(F32)
     sub = lax.broadcasted_iota(jnp.int32, (SUB, D), 0)
@@ -398,10 +398,10 @@
             return ref.at[n * many : (n + 1) * many]
         return ref.at[:, n] if which == 0 else ref.at[:, 2 * n : 2 * n + 2]
 
-    def core_half(which, chunk, q):
+    def core_half(which, chunk):
         if chunk < 2:
-            return weights.at[chunk, which * 8 : which * 8 + 8, pl.ds(q * ZP, ZP)]
-        return outs.at[slice(*OUT_PART[chunk]), :, q, which * 2 : which * 2 + 2]
+            return weights.at[chunk, which * 8 : which * 8 + 8]
+        return outs.at[slice(*OUT_PART[chunk]), :, :, which * 2 : which * 2 + 2]
 
     def by_core(act):
         pl.when(c == 0)(lambda: act(0))
@@ -421,44 +421,54 @@
             ref = piece(which, chunk, q, 0)
             peer = y_peer if which == 0 else x_peer
             for off in (1, 3) if ring else (2, 1, 3):
-                copy(ref, ref, p_s.at[chunk], p2_r.at[chunk, q, off - 1], peer(off)).start()
-            copy(ref, ref, p_s.at[chunk], f_r.at[chunk, q], partner).start()
+                copy(ref, ref, p_s.at[chunk], p2_r.at[chunk, q, 1 - off % 2], peer(off)).start()
+            pass_on(which, chunk, q, 0)
 
         by_core(act)
 
     def pass_on(which, chunk, q, off):
         ref = piece(which, chunk, q, off)
-        copy(ref, ref, p_s.at[chunk], p2_r.at[chunk, q, off - 1], partner).wait_recv()
-        copy(ref, ref, p_s.at[chunk], f_r.at[chunk, q], partner).start()
-
-    def after_step2(chunk, q):
-        def act(which):
-            for off in (1, 3, 2):
-                pass_on(which, chunk, q, off)
-
-        by_core(act)
+        copy(ref, ref, p_s.at[chunk], f_r.at[chunk], partner).start()
+
+    def got_near(chunk, q):
+        ref = group(chunk, 8 * ZP, 8)
+        copy(ref, ref, p_s.at[chunk], p2_r.at[chunk, q, 0], partner).wait_recv()
 
     def after_near(chunk, q):
         def act(which):
             peer = y_peer if which == 0 else x_peer
             for off in (1, 3):
-                pass_on(which, chunk, q, off)
                 on = piece_part(which, chunk, q, off, off // 2)
                 copy(on, on, p_s.at[chunk], p2_r.at[chunk, q, 1], peer(off)).start()
-
+            for off in (1, 3):
+                pass_on(which, chunk, q, off)
+
+        got_near(chunk, q)
         by_core(act)
 
     def after_far(chunk, q):
-        by_core(lambda which: pass_on(which, chunk, q, 2))
+        def act(which):
+            ref = piece(which, chunk, q, 2)
+            copy(ref, ref, p_s.at[chunk], p2_r.at[chunk, q, 1], partner).wait_recv()
+            pass_on(which, chunk, q, 2)
+
+        by_core(act)
+
+    def after_step2(chunk, q):
+        def act(which):
+            pass_on(which, chunk, q, 1)
+            pass_on(which, chunk, q, 3)
+
+        got_near(chunk, q)
+        by_core(act)
+        after_far(chunk, q)
 
     def after_forward(chunk):
-        for q in range(ZS // ZP):
-
-            def act(which, q=q):
-                ref = core_half(1 - which, chunk, q)
-                copy(ref, ref, p_s.at[chunk], f_r.at[chunk, q], partner).wait_recv()
-
-            by_core(act)
+        def act(which):
+            ref = core_half(1 - which, chunk)
+            copy(ref, ref, p_s.at[chunk], f_r.at[chunk], partner).wait_recv()
+
+        by_core(act)
 
     q0, q1 = zq, zq + 1 - 2 * (zq % 2)
     q2 = 2 * (1 - zq // 2)
@@ -517,17 +527,19 @@
         codes_third()
         near_of(*own)
         z_of(*half(IN0))
-        ring1_of(*sib)
+        step1_of(*sib[:1])
+        ring1_of(*sib[1:])
         for chunk in ORDER[1:]:
             z_to(chunk, 2 * ZP, ZS)
         far_of(*own)
         step1_of(*half(IN0))
         z_of(*half(OUT0))
-        near_of(*sib)
+        step2_of(*sib[:1])
+        near_of(*sib[1:])
         z_of(*half(IN1))
         step1_of(*half(OUT0))
         step1_of(*half(IN1))
-        far_of((q1, IN0), (q1, OUT0))
+        far_of((q1, OUT0))
         step2_of(*half(IN0))
         z_of(*half(OUT1))
         far_of((q1, IN1), (q1, OUT1))
@@ -560,9 +572,11 @@
         far_of(*both(IN1))
         step2_of(*half(IN0))
 
+    for pair in range(4):
+        project(0, 4 * c + pair, weights, normed, proj)
     after_forward(IN0)
-    for pair in range(8):
-        project(0, pair, weights, normed, proj)
+    for pair in range(4):
+        project(0, 4 - 4 * c + pair, weights, normed, proj)
 
     if_late(lambda: near_of(*both(OUT1)))
     step2_of(*half(OUT0))
@@ -572,18 +586,20 @@
     step2_of(*half(IN1))
     after_forward(OUT0)
     add_out(0, outs, 0, proj, attn, x, normed)
+    for pair in range(4):
+        project(1, 4 * c + pair, weights, normed, proj)
     after_forward(IN1)
-    for pair in range(8):
-        project(1, pair, weights, normed, proj)
+    for pair in range(4):
+        project(1, 4 - 4 * c + pair, weights, normed, proj)
     if_late(lambda: far_of(*both(OUT1)))
     step2_of(*half(OUT1))
     for head in range(HEADS):
         attend(head, proj, attn)
     codes_last()
     after_forward(OUT1)
-    add_out(1, outs, 1, proj, attn, x, normed)
-
-    make_tables(outs, x, codebook, tables)
+    means = add_out(1, outs, 1, proj, attn, x, normed)
+
+    make_tables(outs, means, codebook, tables)
     score(tables, codes_got, cand, counts, out)
 
     for t in trades:
@@ -639,8 +655,8 @@
             dma((4, 4)),
             dma((4,)),
             dma((4, 4)),
-            dma((4, 4, 3)),
-            dma((4, 4)),
+            dma((4, 4, 2)),
+            dma((4,)),
             dma(()),
             dma((3,)),
         ],

time: 49 us -> 48.5 us (0.990)
  Pallas kernels: 48.3 us -> 47.7 us
    pallas_call x1, Pallas kernels: 48.3 us -> 47.7 us  [body(): pl.pallas_call(kernel, out_shape=pltpu.VMEM((INTR, ITEMS, CAND, BS), F32)...]
where the time goes in v6:
time: 48.5 us; the launch traced here: 48.3 us
  Pallas kernels  47.7 us (98%)
  local copies, waits for them, and re-layouts  0.63 us (1%)
    pallas_call x1, Pallas kernels, body(): pl.pallas_call(kernel, out_shape=pltpu.VMEM((INTR, ITEMS, CAND, BS), F32)...  47.7 us

profile of v6, /device:TPU:1, one launch (start us, length us, event | category | flops | bytes accessed | tf_op | source)
XLA Modules:
  0.0 48.3 jit_solution(5261424831989104787)
XLA Ops:
  0.0 47.7 %encode_and_score.1 = f32[4,8,4,128]{3,2,1,0:T(4,128)S(1)} custom-call(bf16[1,512,512]{2,1,0:T(8,128)(2,1)} %hist_h.1, s32[1,512]{1,0:T(1,128)} %act_h.1, bf16[16,512]{1,0:T(8,128)(2,1)} %table_h.1, bf16[2,8,2048]{2,1,0:T(8,128)(2,1)} %win_h.1, bf16[2,8,512]{2,1,0:T(8,128)(2,1)} %wout_h.1, bf16[8,512]{1,0:T(8,128)(2,1)} %wint_h.1, ...), custom_call_target="tpu_custom_call" | custom-call | tf_op jit(solution)/shard_map/encode_and_score/pallas_call | solution.py:630
  47.7 0.6 %copy.12 = f32[1,4,8,4,128]{4,3,2,1,0:T(4,128)} copy(f32[1,4,8,4,128]{4,3,2,1,0:T(4,128)S(1)} %bitcast.4) | data formatting | bytes 131072

commit v7 on v6

--- a/solution.py
+++ b/solution.py
@@ -551,14 +551,15 @@
     def _():
         z_of(*both(IN0))
         z_of(*both(OUT0))
-        step1_of(*both(IN0))
+        ring1_of(*both(IN0))
         z_of(*both(IN1))
         ring1_of(*both(OUT0))
         codes_third()
-        step2_of(*both(IN0))
+        near_of(*both(IN0))
         ring1_of(*both(IN1))
         z_of(*half(IN0))
         near_of(*both(OUT0))
+        far_of(*both(IN0))
         z_of(*both(OUT1))
         step1_of(*half(IN0))
         near_of(*both(IN1))

time: 48.5 us -> 48.5 us (level)
  no operation moved by 1% of the time
where the time goes in v7:
time: 48.5 us; the launch traced here: 48.3 us
  Pallas kernels  47.7 us (98%)
  local copies, waits for them, and re-layouts  0.63 us (1%)
    pallas_call x1, Pallas kernels, body(): pl.pallas_call(kernel, out_shape=pltpu.VMEM((INTR, ITEMS, CAND, BS), F32)...  47.7 us

profile of v7, /device:TPU:1, one launch (start us, length us, event | category | flops | bytes accessed | tf_op | source)
XLA Modules:
  0.0 48.3 jit_solution(18183218371938560949)
XLA Ops:
  0.0 47.7 %encode_and_score.1 = f32[4,8,4,128]{3,2,1,0:T(4,128)S(1)} custom-call(bf16[1,512,512]{2,1,0:T(8,128)(2,1)} %hist_h.1, s32[1,512]{1,0:T(1,128)} %act_h.1, bf16[16,512]{1,0:T(8,128)(2,1)} %table_h.1, bf16[2,8,2048]{2,1,0:T(8,128)(2,1)} %win_h.1, bf16[2,8,512]{2,1,0:T(8,128)(2,1)} %wout_h.1, bf16[8,512]{1,0:T(8,128)(2,1)} %wint_h.1, ...), custom_call_target="tpu_custom_call" | custom-call | tf_op jit(solution)/shard_map/encode_and_score/pallas_call | solution.py:631
  47.7 0.6 %copy.12 = f32[1,4,8,4,128]{4,3,2,1,0:T(4,128)} copy(f32[1,4,8,4,128]{4,3,2,1,0:T(4,128)S(1)} %bitcast.4) | data formatting | bytes 131072
